TPU v7x, 512 devices: a whole 4x8x8 slice. The times are simulated.
512 devices in a mesh: dp: 4 (over y_lo, core), ctx: 32 (over z, y_hi), tp: 4 (over x).
Axes of the slice: x: 4, y: 8 (y_hi: 4, y_lo: 2; y = y_hi * 2 + y_lo), z: 8, core: 2. Of those that a mesh axis runs over, the one named last changes fastest.
Arguments:
- queries: bfloat16 [16384, 4096], P(('dp', 'ctx'), 'tp'), parts along dimension 0, may hold values from -120 to 120
- keys: bfloat16 [16384, 512], P(('dp', 'ctx'), 'tp'), parts along dimension 0, may hold values from -12 to 12
- values: bfloat16 [16384, 512], P(('dp', 'ctx'), 'tp'), parts along dimension 0, may hold values from -20 to 20
- readout: bfloat16 [4096, 1536], P('tp'), may hold values from -8 to 8
- token_ids: int32 [16384], P(('dp', 'ctx')), parts along dimension 0, may hold values from 0 to 1535
- stored_logp: float32 [16384], P(('dp', 'ctx')), parts along dimension 0, may hold values from -12 to -0.5
- span_order: int32 [256], P('dp'), parts along dimension 0, may hold values from 0 to 63, each once
Outputs:
- attended: bfloat16 [16384, 4096], P(('dp', 'ctx'), 'tp'), parts along dimension 0
- log_ratio: float32 [16384], P(('dp', 'ctx')), parts along dimension 0
There are 4 independent parts, one for each index of `dp`. A program takes and returns all parts, laid end to end along the dimension named above; an argument that names none is the same for every part. Nothing has to cross between parts.
Inputs may be any that keep to these rules, and one draw needn't show every extreme that they name: `span_order`: each block index appears in exactly one slot.
All inputs are finite; a program needn't handle non-finite values.
Results may differ from a plain program's by a relative error of at most 0.006.
Values may be sent and summed in bfloat16 or wider, within the bound.
No kernel may reach another device: no remote copies, remote signals or barrier semaphores. Data moves between devices by JAX's collectives and lax.ppermute only.
A program may use at most 64 MiB of HBM per device.

v0:
```python
import math

import jax
import jax.numpy as jnp
from jax import lax
from jax.sharding import PartitionSpec as P

HEAD_SIZE = 128


floor_value = -1e30


def row_positions(span_order, start, row_count, halved_row_count):
    first_slot = start // halved_row_count
    span_ids = lax.dynamic_slice_in_dim(span_order, first_slot, row_count // halved_row_count, 0)
    offsets = jnp.arange(halved_row_count, dtype=jnp.int32)
    return (span_ids[:, None] * halved_row_count + offsets[None, :]).reshape(-1)


def body(queries, keys, values, readout, token_ids, stored_logp, span_order):
    tok_rows = queries.shape[0]
    halved_row_count = tok_rows // 2
    kv_local = keys.shape[1] // HEAD_SIZE
    query_group_ratio = queries.shape[1] // keys.shape[1]
    score_scale = 1.0 / math.sqrt(HEAD_SIZE)
    device_ctx = lax.axis_index("ctx")
    query_pos = row_positions(span_order, device_ctx * tok_rows, tok_rows, halved_row_count)
    query_heads = queries.reshape(tok_rows, kv_local, query_group_ratio, HEAD_SIZE)

    def compute(state, key_blk, value_blk, key_pos):
        run_peak, run_total, run_accum = state
        scores = (
            jnp.einsum("qgrd,kgd->qgrk", query_heads, key_blk, preferred_element_type=jnp.float32)
            * score_scale
        )
        visible = key_pos[None, None, None, :] <= query_pos[:, None, None, None]
        scores = jnp.where(visible, scores, floor_value)
        new_peak = jnp.maximum(run_peak, jnp.max(scores, axis=-1))
        weights = jnp.where(visible, jnp.exp(scores - new_peak[..., None]), 0.0)
        factor = jnp.exp(run_peak - new_peak)
        run_total = run_total * factor + jnp.sum(weights, axis=-1)
        mixed = jnp.einsum(
            "qgrk,kgd->qgrd",
            weights.astype(jnp.bfloat16),
            value_blk,
            preferred_element_type=jnp.float32,
        )
        run_accum = run_accum * factor[..., None] + mixed
        return (new_peak, run_total, run_accum)

    def attend_block(running, block_data):
        key_blk, value_blk, key_pos = block_data
        running = compute(running, key_blk, value_blk, key_pos)
        return (running, None)

    start_state = (
        jnp.full((tok_rows, kv_local, query_group_ratio), floor_value, jnp.float32),
        jnp.zeros((tok_rows, kv_local, query_group_ratio), jnp.float32),
        jnp.zeros((tok_rows, kv_local, query_group_ratio, HEAD_SIZE), jnp.float32),
    )
    every_key, every_value = (
        lax.all_gather(keys, "ctx", axis=0, tiled=True),
        lax.all_gather(values, "ctx", axis=0, tiled=True),
    )
    running = start_state
    row_count = every_key.shape[0]
    block_rows = math.gcd(row_count, 512)
    block_count = row_count // block_rows
    key_pos = row_positions(span_order, 0, row_count, halved_row_count)
    blocked = (
        every_key.reshape(block_count, block_rows, kv_local, HEAD_SIZE),
        every_value.reshape(block_count, block_rows, kv_local, HEAD_SIZE),
        key_pos.reshape(block_count, block_rows),
    )
    running, _ = lax.scan(attend_block, running, blocked)
    run_peak, run_total, run_accum = running
    attended = (
        (run_accum / run_total[..., None])
        .reshape(tok_rows, kv_local * query_group_ratio * HEAD_SIZE)
        .astype(jnp.bfloat16)
    )
    vocab_local = readout.shape[1] // lax.axis_size("tp")
    logits = lax.psum_scatter(
        lax.dot_general(
            readout, attended, (((0,), (1,)), ((), ())), preferred_element_type=jnp.float32
        ),
        "tp",
        scatter_dimension=0,
        tiled=True,
    )
    vocab_start = lax.axis_index("tp") * vocab_local
    hit = jnp.arange(vocab_local, dtype=jnp.int32)[:, None] == (token_ids - vocab_start)[None, :]
    local_target = jnp.sum(jnp.where(hit, logits, 0.0), axis=0)
    local_peak = jnp.max(logits, axis=0)
    peak_all = lax.pmax(local_peak, "tp")
    local_mass = jnp.sum(jnp.exp(logits - peak_all[None, :]), axis=0)
    mass_all, target = lax.psum((local_mass, local_target), "tp")
    log_ratio = target - (peak_all + jnp.log(mass_all)) - stored_logp
    return (attended, log_ratio)


def solution(mesh):
    return jax.shard_map(
        body,
        mesh=mesh,
        in_specs=(
            P(("dp", "ctx"), "tp"),
            P(("dp", "ctx"), "tp"),
            P(("dp", "ctx"), "tp"),
            P("tp", None),
            P(("dp", "ctx")),
            P(("dp", "ctx")),
            P("dp"),
        ),
        out_specs=(P(("dp", "ctx"), "tp"), P(("dp", "ctx"))),
        check_vma=False,
    )
```

profile of v0, /device:TPU:16, one launch (start us, length us, event | category | flops | bytes accessed | tf_op | source)
XLA Modules:
  0.0 289.8 jit_solution(4714171639816127263)
XLA Ops:
  8.8 1.8 copy.12
  13.4 85.2 %all-gather.3.cloned.1.call-done = bf16[4096,128]{1,0:T(8,128)(2,1)} async-done(((bf16[128,128]{1,0:T(8,128)(2,1)}), bf16[4096,128]{1,0:T(8,128)(2,1)}) %all-gather.3.cloned.1.call-update) | async-done | bytes 1048592 | tf_op jit(solution)/shard_map/all_gather | solution.py:63
  98.6 82.4 %all-gather.5.cloned.1.call-done = bf16[4096,128]{1,0:T(8,128)(2,1)} async-done(((bf16[128,128]{1,0:T(8,128)(2,1)}), bf16[4096,128]{1,0:T(8,128)(2,1)}) %all-gather.5.cloned.1.call-update) | async-done | bytes 1048592 | tf_op jit(solution)/shard_map/all_gather | solution.py:64
  181.0 55.3 %while.15 = (s32[]{:T(128)}, f32[128,1,8]{0,2,1:T(8,128)S(1)}, f32[128,1,8]{0,2,1:T(8,128)S(1)}, f32[128,1,8,128]{0,3,2,1:T(8,128)}, s32[8,512]{1,0:T(8,128)S(1)...) while((s32[]{:T(128)}, f32[128,1,8]{0,2,1:T(8,128)S(1)}, ...), condition=%wide.region_3.4_spmd.clone, body=%wide.region_0.3_spmd.clone.sunk | while | flops 275716224 | bytes 16589985 | solution.py:76
  181.3 2.7 fusion.35
  184.0 3.2 %fusion.38 = f32[128,1,8,128]{0,3,2,1:T(8,128)} fusion(f32[512,128,8]{1,0,2:T(8,128)} %get-tuple-element.181, f32[128,8]{0,1:T(8,128)S(1)} %bitcast.86, pred[128,512]{0,1:T(8,128)(4,1)S(1)} %broadcast_compare_fusion.2, f32[128,1,8,128]{0,3,2,1:T(8,128)} %get-tuple-element.197, f32[128,8]{0,1:T(8,128)S(1)} %get-tuple-element.182, pred[]{:T(512)S(6)} %compare.5, ...), kind=kOutput, calls=%fused_computation.7.clone.1 | convolution fusion | flops 137232384 | bytes 3351041 | tf_op jit(solution)/shard_map/while/body/eval_jaxpr/qgrk,kgd->qgrd/dot_general | solution.py:43
  188.1 2.7 fusion.35
  190.8 3.3 %fusion.38 = f32[128,1,8,128]{0,3,2,1:T(8,128)} fusion(f32[512,128,8]{1,0,2:T(8,128)} %get-tuple-element.181, f32[128,8]{0,1:T(8,128)S(1)} %bitcast.86, pred[128,512]{0,1:T(8,128)(4,1)S(1)} %broadcast_compare_fusion.2, f32[128,1,8,128]{0,3,2,1:T(8,128)} %get-tuple-element.197, f32[128,8]{0,1:T(8,128)S(1)} %get-tuple-element.182, pred[]{:T(512)S(6)} %compare.5, ...), kind=kOutput, calls=%fused_computation.7.clone.1 | convolution fusion | flops 137232384 | bytes 3351041 | tf_op jit(solution)/shard_map/while/body/eval_jaxpr/qgrk,kgd->qgrd/dot_general | solution.py:43
  195.0 2.7 fusion.35
  197.8 3.3 %fusion.38 = f32[128,1,8,128]{0,3,2,1:T(8,128)} fusion(f32[512,128,8]{1,0,2:T(8,128)} %get-tuple-element.181, f32[128,8]{0,1:T(8,128)S(1)} %bitcast.86, pred[128,512]{0,1:T(8,128)(4,1)S(1)} %broadcast_compare_fusion.2, f32[128,1,8,128]{0,3,2,1:T(8,128)} %get-tuple-element.197, f32[128,8]{0,1:T(8,128)S(1)} %get-tuple-element.182, pred[]{:T(512)S(6)} %compare.5, ...), kind=kOutput, calls=%fused_computation.7.clone.1 | convolution fusion | flops 137232384 | bytes 3351041 | tf_op jit(solution)/shard_map/while/body/eval_jaxpr/qgrk,kgd->qgrd/dot_general | solution.py:43
  202.0 2.7 fusion.35
  204.7 3.3 %fusion.38 = f32[128,1,8,128]{0,3,2,1:T(8,128)} fusion(f32[512,128,8]{1,0,2:T(8,128)} %get-tuple-element.181, f32[128,8]{0,1:T(8,128)S(1)} %bitcast.86, pred[128,512]{0,1:T(8,128)(4,1)S(1)} %broadcast_compare_fusion.2, f32[128,1,8,128]{0,3,2,1:T(8,128)} %get-tuple-element.197, f32[128,8]{0,1:T(8,128)S(1)} %get-tuple-element.182, pred[]{:T(512)S(6)} %compare.5, ...), kind=kOutput, calls=%fused_computation.7.clone.1 | convolution fusion | flops 137232384 | bytes 3351041 | tf_op jit(solution)/shard_map/while/body/eval_jaxpr/qgrk,kgd->qgrd/dot_general | solution.py:43
  208.9 2.7 fusion.35
  211.6 3.3 %fusion.38 = f32[128,1,8,128]{0,3,2,1:T(8,128)} fusion(f32[512,128,8]{1,0,2:T(8,128)} %get-tuple-element.181, f32[128,8]{0,1:T(8,128)S(1)} %bitcast.86, pred[128,512]{0,1:T(8,128)(4,1)S(1)} %broadcast_compare_fusion.2, f32[128,1,8,128]{0,3,2,1:T(8,128)} %get-tuple-element.197, f32[128,8]{0,1:T(8,128)S(1)} %get-tuple-element.182, pred[]{:T(512)S(6)} %compare.5, ...), kind=kOutput, calls=%fused_computation.7.clone.1 | convolution fusion | flops 137232384 | bytes 3351041 | tf_op jit(solution)/shard_map/while/body/eval_jaxpr/qgrk,kgd->qgrd/dot_general | solution.py:43
  215.8 2.7 fusion.35
  218.5 3.3 %fusion.38 = f32[128,1,8,128]{0,3,2,1:T(8,128)} fusion(f32[512,128,8]{1,0,2:T(8,128)} %get-tuple-element.181, f32[128,8]{0,1:T(8,128)S(1)} %bitcast.86, pred[128,512]{0,1:T(8,128)(4,1)S(1)} %broadcast_compare_fusion.2, f32[128,1,8,128]{0,3,2,1:T(8,128)} %get-tuple-element.197, f32[128,8]{0,1:T(8,128)S(1)} %get-tuple-element.182, pred[]{:T(512)S(6)} %compare.5, ...), kind=kOutput, calls=%fused_computation.7.clone.1 | convolution fusion | flops 137232384 | bytes 3351041 | tf_op jit(solution)/shard_map/while/body/eval_jaxpr/qgrk,kgd->qgrd/dot_general | solution.py:43
  222.7 2.7 fusion.35
  225.5 3.3 %fusion.38 = f32[128,1,8,128]{0,3,2,1:T(8,128)} fusion(f32[512,128,8]{1,0,2:T(8,128)} %get-tuple-element.181, f32[128,8]{0,1:T(8,128)S(1)} %bitcast.86, pred[128,512]{0,1:T(8,128)(4,1)S(1)} %broadcast_compare_fusion.2, f32[128,1,8,128]{0,3,2,1:T(8,128)} %get-tuple-element.197, f32[128,8]{0,1:T(8,128)S(1)} %get-tuple-element.182, pred[]{:T(512)S(6)} %compare.5, ...), kind=kOutput, calls=%fused_computation.7.clone.1 | convolution fusion | flops 137232384 | bytes 3351041 | tf_op jit(solution)/shard_map/while/body/eval_jaxpr/qgrk,kgd->qgrd/dot_general | solution.py:43
  229.7 2.7 fusion.35
  232.4 3.3 %fusion.38 = f32[128,1,8,128]{0,3,2,1:T(8,128)} fusion(f32[512,128,8]{1,0,2:T(8,128)} %get-tuple-element.181, f32[128,8]{0,1:T(8,128)S(1)} %bitcast.86, pred[128,512]{0,1:T(8,128)(4,1)S(1)} %broadcast_compare_fusion.2, f32[128,1,8,128]{0,3,2,1:T(8,128)} %get-tuple-element.197, f32[128,8]{0,1:T(8,128)S(1)} %get-tuple-element.182, pred[]{:T(512)S(6)} %compare.5, ...), kind=kOutput, calls=%fused_computation.7.clone.1 | convolution fusion | flops 137232384 | bytes 3351041 | tf_op jit(solution)/shard_map/while/body/eval_jaxpr/qgrk,kgd->qgrd/dot_general | solution.py:43
  237.4 1.5 convolution_bitcast_fusion.1
  239.8 23.4 %reduce-scatter.2.cloned.1.call-done = f32[384,128]{0,1:T(8,128)} async-done(((f32[1536,128]{0,1:T(8,128)}), f32[384,128]{0,1:T(8,128)}) %reduce-scatter.2.cloned.1.call-update) | async-done | bytes 196624 | tf_op jit(solution)/shard_map/reduce_scatter | solution.py:84
  264.2 8.2 %pmax.7 = f32[128]{0:T(128)S(1)} all-reduce(f32[128]{0:T(128)S(1)} %reduce_max.20), channel_id=1, replica_groups=mesh['dp'=4,'ctx'=32,'tp'=4] {'tp'}, use_global_device_ids=true, to_apply=%region_8.9 | all-reduce | flops 128 | bytes 1024 | tf_op jit(solution)/shard_map/pmax | solution.py:96
  273.5 9.3 %all-reduce = (f32[128]{0:T(128)S(1)}, f32[128]{0:T(128)S(1)}) all-reduce(f32[128]{0:T(128)S(1)} %get-tuple-element.95, f32[128]{0:T(128)S(1)} %get-tuple-element.94), channel_id=1, replica_groups=mesh['dp'=4,'ctx'=32,'tp'=4] {'tp'}, use_global_device_ids=true, to_apply=%region_6.7 | all-reduce | flops 256 | bytes 2048 | tf_op jit(solution)/shard_map/psum | solution.py:98
  (110 shorter events, 15.7 us)
Async XLA Ops:
  7.2 230.2 %copy-start = (bf16[1024,1536]{1,0:T(8,128)(2,1)S(1)}, bf16[1024,1536]{1,0:T(8,128)(2,1)}, u32[]{:S(2)}) copy-start(bf16[1024,1536]{1,0:T(8,128)(2,1)} %param.12) | copy-start | bytes 9437188
  7.2 91.4 %all-gather.3.cloned.1.call-start = ((), (), s32[]{:S(2)}) async-start(), calls=%async_computation.1 | async-start | bytes 1081344 | tf_op jit(solution)/shard_map/all_gather | solution.py:63
  7.9 173.1 %all-gather.5.cloned.1.call-start = ((), (), s32[]{:S(2)}) async-start(), calls=%async_computation.2 | async-start | bytes 1081344 | tf_op jit(solution)/shard_map/all_gather | solution.py:64
  8.7 254.5 %reduce-scatter.2.cloned.1.call-start = ((), (), s32[]{:S(2)}) async-start(), calls=%async_computation.3 | async-start | bytes 983040 | tf_op jit(solution)/shard_map/reduce_scatter | solution.py:84
  184.0 3.3 %copy-start.1 = (f32[512,128,8]{1,0,2:T(8,128)S(1)}, f32[512,128,8]{1,0,2:T(8,128)}, u32[]{:S(2)}) copy-start(f32[512,128,8]{1,0,2:T(8,128)} %get-tuple-element.181) | copy-start | bytes 6291460 | tf_op jit(solution)/shard_map/while
  190.8 3.3 %copy-start.1 = (f32[512,128,8]{1,0,2:T(8,128)S(1)}, f32[512,128,8]{1,0,2:T(8,128)}, u32[]{:S(2)}) copy-start(f32[512,128,8]{1,0,2:T(8,128)} %get-tuple-element.181) | copy-start | bytes 6291460 | tf_op jit(solution)/shard_map/while
  197.8 3.3 %copy-start.1 = (f32[512,128,8]{1,0,2:T(8,128)S(1)}, f32[512,128,8]{1,0,2:T(8,128)}, u32[]{:S(2)}) copy-start(f32[512,128,8]{1,0,2:T(8,128)} %get-tuple-element.181) | copy-start | bytes 6291460 | tf_op jit(solution)/shard_map/while
  204.7 3.3 %copy-start.1 = (f32[512,128,8]{1,0,2:T(8,128)S(1)}, f32[512,128,8]{1,0,2:T(8,128)}, u32[]{:S(2)}) copy-start(f32[512,128,8]{1,0,2:T(8,128)} %get-tuple-element.181) | copy-start | bytes 6291460 | tf_op jit(solution)/shard_map/while
  211.6 3.3 %copy-start.1 = (f32[512,128,8]{1,0,2:T(8,128)S(1)}, f32[512,128,8]{1,0,2:T(8,128)}, u32[]{:S(2)}) copy-start(f32[512,128,8]{1,0,2:T(8,128)} %get-tuple-element.181) | copy-start | bytes 6291460 | tf_op jit(solution)/shard_map/while
  218.5 3.3 %copy-start.1 = (f32[512,128,8]{1,0,2:T(8,128)S(1)}, f32[512,128,8]{1,0,2:T(8,128)}, u32[]{:S(2)}) copy-start(f32[512,128,8]{1,0,2:T(8,128)} %get-tuple-element.181) | copy-start | bytes 6291460 | tf_op jit(solution)/shard_map/while
  225.5 3.3 %copy-start.1 = (f32[512,128,8]{1,0,2:T(8,128)S(1)}, f32[512,128,8]{1,0,2:T(8,128)}, u32[]{:S(2)}) copy-start(f32[512,128,8]{1,0,2:T(8,128)} %get-tuple-element.181) | copy-start | bytes 6291460 | tf_op jit(solution)/shard_map/while
  232.4 3.3 %copy-start.1 = (f32[512,128,8]{1,0,2:T(8,128)S(1)}, f32[512,128,8]{1,0,2:T(8,128)}, u32[]{:S(2)}) copy-start(f32[512,128,8]{1,0,2:T(8,128)} %get-tuple-element.181) | copy-start | bytes 6291460 | tf_op jit(solution)/shard_map/while
  237.4 1.5 copy-start.3
  237.4 45.4 %copy-start.2 = (f32[128]{0:T(128)S(1)}, f32[128]{0:T(128)}, u32[]{:S(2)}) copy-start(f32[128]{0:T(128)} %param.14) | copy-start | bytes 1540
Sparse Core Ops, SparseCore 0:
  11.2 87.3 all-gather.2
  101.7 79.1 all-gather.4
  239.0 24.0 reduce-scatter.1
where the time goes:
time: 290 us
  waiting for transfers between devices  192 us (66%)
  matrix products  49.6 us (17%)
  blocking collectives  17.5 us (6%)
  between operations  13.9 us (5%)
  other arithmetic  11.1 us (4%)
  local copies, waits for them, and re-layouts  4.88 us (2%)
    all_gather x1, waiting for transfers between devices, body(): lax.all_gather(keys, 'ctx', axis=0, tiled=True)  85.2 us
    all_gather x1, waiting for transfers between devices, body(): lax.all_gather(values, 'ctx', axis=0, tiled=True)  82.4 us
    dot_general x8, matrix products, compute(): jnp.einsum('qgrk,kgd->qgrd', weights.astype(jnp.bfloat16), value_blk, pre...  26.5 us
    reduce_scatter x1, waiting for transfers between devices, body(): lax.psum_scatter(lax.dot_general(readout, attended, (((0,), (1,)), ((), (...  23.4 us
    dot_general x8, matrix products, compute(): jnp.einsum('qgrd,kgd->qgrk', query_heads, key_blk, preferred_element_type...  21.6 us
    psum x1, blocking collectives, body(): mass_all, target = lax.psum((local_mass, local_target), 'tp')  9.26 us
    pmax x1, blocking collectives, body(): peak_all = lax.pmax(local_peak, 'tp')  8.24 us
  transfers between devices with their start and end apart: 3, of which 3 were waited for; matrix products, arithmetic and copies ran while one was open for 2% of the time, Pallas kernels for 0%

commit v1 on v0

v1 whole, which is shorter than its diff:
```python
import functools
import math

import jax
import jax.numpy as jnp
from jax import lax
from jax.experimental import pallas as pl
from jax.experimental.pallas import tpu as pltpu
from jax.sharding import PartitionSpec as P

HEAD = 128
Z = 8
Y = 4
TP = 4
SPAN = 64
ROW_TILE = 256
EXP2_SCALE = math.log2(math.e) / math.sqrt(HEAD)
MASKED = -1e30
COST = 4
Y_GROUPS = [[z * Y + y for y in range(Y)] for z in range(Z)]


def swap_z(x, odd):
    pairs = []
    for z in range(Z):
        partner = (z + (1 if z % 2 == odd else -1)) % Z
        pairs += [(z * Y + y, partner * Y + y) for y in range(Y)]
    return lax.ppermute(x, "ctx", pairs)


VMEM = pl.BlockSpec(memory_space=pltpu.VMEM)
SMEM = pl.BlockSpec(memory_space=pltpu.SMEM)
HBM = pl.BlockSpec(memory_space=pltpu.HBM)


def block(dz):
    return [(dz, y) for y in range(Y)]


def ring_order():
    order = block(0)
    for step in range(1, Z // 2):
        dz = step if step % 2 else -step
        order += block(dz) + block(-dz)
    return order + block(Z // 2)


def pack_kernel(k_ref, v_ref, out_ref, sems):
    copies = []
    for j in range(Y):
        copies.append(pltpu.make_async_copy(k_ref, out_ref.at[j, :, pl.ds(0, HEAD)], sems.at[2 * j]))
        copies.append(pltpu.make_async_copy(v_ref, out_ref.at[j, :, pl.ds(HEAD, HEAD)], sems.at[2 * j + 1]))
    for copy in copies:
        copy.start()
    for copy in copies:
        copy.wait()


def pack(keys, values):
    return pl.pallas_call(
        pack_kernel,
        out_shape=jax.ShapeDtypeStruct((Y, keys.shape[0], 2 * HEAD), keys.dtype),
        in_specs=[HBM] * 2,
        out_specs=VMEM,
        scratch_shapes=[pltpu.SemaphoreType.DMA((2 * Y,))],
        name="pack",
    )(keys, values)


def prep_kernel(ids, order, q_ref, q_all, bias_ref, sem):
    heads = q_ref.shape[1] // HEAD
    rows = q_ref.shape[0]
    copies = []
    for h in range(heads):
        copies.append(
            pltpu.make_async_copy(
                q_ref.at[:, pl.ds(h * HEAD, HEAD)], q_all.at[pl.ds(h * rows, rows), pl.ds(0, HEAD)], sem.at[h]
            )
        )
        copies[h].start()
    eye = (
        lax.broadcasted_iota(jnp.int32, (HEAD, HEAD), 0) == lax.broadcasted_iota(jnp.int32, (HEAD, HEAD), 1)
    ).astype(jnp.bfloat16)
    for h in range(heads):
        q_all[h * rows : (h + 1) * rows, HEAD:] = eye
    me = ids[0]
    z = me // Y
    sign = 1 - 2 * (z % 2)
    row = lax.broadcasted_iota(jnp.int32, (SPAN, 2 * SPAN), 1)
    key = lax.broadcasted_iota(jnp.int32, (SPAN, 2 * SPAN), 0)
    row_pos = jnp.where(row < SPAN, order[2 * me] * SPAN + row, order[2 * me + 1] * SPAN + row - SPAN)
    lead = row_pos - key
    for i, (dz, y) in enumerate(ring_order()):
        src = ((z + sign * dz + Z) % Z) * Y + y
        for half in range(2):
            at = (2 * i + half) * SPAN
            visible = lead >= order[2 * src + half] * SPAN
            bias_ref[at : at + SPAN, :] = jnp.where(visible, 0.0, MASKED).astype(jnp.bfloat16)
    for copy in copies:
        copy.wait()


def prep(ids, order, queries):
    rows, width = queries.shape
    return pl.pallas_call(
        prep_kernel,
        out_shape=[
            jax.ShapeDtypeStruct((rows * (width // HEAD), 2 * HEAD), jnp.bfloat16),
            jax.ShapeDtypeStruct((Z * Y * rows, rows), jnp.bfloat16),
        ],
        in_specs=[SMEM, SMEM, HBM],
        out_specs=[VMEM, VMEM],
        scratch_shapes=[pltpu.SemaphoreType.DMA((width // HEAD,))],
        cost_estimate=pl.CostEstimate(flops=2 * 10**9, bytes_accessed=2 * 2**20, transcendentals=0),
        compiler_params=pltpu.CompilerParams(vmem_limit_bytes=16 * 2**20),
        name="prep",
    )(ids, order, queries)


def attend_kernel(start, n_kv, first, last, q_all, bias_ref, *refs):
    kv_refs, refs = refs[:n_kv], refs[n_kv:]
    if not first:
        acc_in, peak_in, refs = refs[0], refs[1], refs[2:]
    if last:
        w_ref, att_ref, part_ref = refs
    else:
        acc_out, peak_out = refs
    total, rows = q_all.shape[0], bias_ref.shape[1]
    k = jnp.concatenate([r[:, :, :HEAD].reshape(-1, HEAD) for r in kv_refs], axis=0)
    v = jnp.concatenate([r[:, :, HEAD:].reshape(-1, HEAD) for r in kv_refs], axis=0)
    k_ext = jnp.concatenate([k, bias_ref[start : start + k.shape[0], :]], axis=1)
    v_ext = jnp.concatenate([v, jnp.ones_like(v)], axis=1)
    for r in range(total // ROW_TILE):
        at = slice(r * ROW_TILE, (r + 1) * ROW_TILE)
        s = lax.dot_general(q_all[at, :], k_ext, (((1,), (1,)), ((), ())), preferred_element_type=jnp.float32)
        peak = jnp.max(s, axis=1, keepdims=True)
        if not first:
            old = peak_in[at, :1]
            peak = jnp.maximum(old, peak)
        p = jnp.exp2((s - peak) * EXP2_SCALE).astype(jnp.bfloat16)
        acc = jnp.dot(p, v_ext, preferred_element_type=jnp.float32)
        if not first:
            acc = acc + acc_in[at, :] * jnp.exp2((old - peak) * EXP2_SCALE)
        if last:
            att = (acc[:, :HEAD] / acc[:, HEAD:]).astype(jnp.bfloat16)
            for i in range(ROW_TILE // rows):
                h = r * ROW_TILE // rows + i
                att_ref[:, h * HEAD : (h + 1) * HEAD] = att[i * rows : (i + 1) * rows, :]
        else:
            acc_out[at, :] = acc
            peak_out[at, :] = jnp.broadcast_to(peak, (ROW_TILE, HEAD))
    if last:
        logits = jnp.dot(att_ref[...], w_ref[...], preferred_element_type=jnp.float32)
        part = rows // TP
        for t in range(TP):
            part_ref[t] = logits[t * part : (t + 1) * part, :].astype(jnp.bfloat16)


def attend(q_all, bias, kvs, start, state=None, readout=None):
    first, last = state is None, readout is not None
    total, rows = q_all.shape[0], bias.shape[1]
    keys = sum(kv.shape[0] * kv.shape[1] for kv in kvs)
    f32, b16 = jnp.float32, jnp.bfloat16
    args = [q_all, bias, *kvs]
    if not first:
        args += list(state)
    if last:
        vocab = readout.shape[1]
        args.append(readout)
        out = [
            jax.ShapeDtypeStruct((rows, total // rows * HEAD), b16),
            jax.ShapeDtypeStruct((TP, rows // TP, vocab), b16),
        ]
    else:
        out = [jax.ShapeDtypeStruct((total, 2 * HEAD), f32), jax.ShapeDtypeStruct((total, HEAD), f32)]
    return pl.pallas_call(
        functools.partial(attend_kernel, start, len(kvs), first, last),
        out_shape=out,
        in_specs=[VMEM] * len(args),
        out_specs=[VMEM] * len(out),
        cost_estimate=pl.CostEstimate(
            flops=COST * 4 * total * keys * 2 * HEAD, bytes_accessed=4 * 2**20, transcendentals=total * keys
        ),
        compiler_params=pltpu.CompilerParams(vmem_limit_bytes=24 * 2**20),
        name="attend_last" if last else "attend",
    )(*args)


def ratio_kernel(ids, part_ref, tok_ref, logp_ref, out_ref):
    f32 = jnp.float32
    _, part, vocab = part_ref.shape
    x = part_ref[0].astype(f32)
    for t in range(1, TP):
        x = x + part_ref[t].astype(f32)
    rows = tok_ref.shape[1]
    start = ids[1] * part
    mine = (
        lax.broadcasted_iota(jnp.int32, (part, rows), 0) + start
        == lax.broadcasted_iota(jnp.int32, (part, rows), 1)
    )
    token = jnp.sum(jnp.where(mine, tok_ref[...].astype(f32), 0.0), axis=1, keepdims=True).astype(jnp.int32)
    hit = lax.broadcasted_iota(jnp.int32, (part, vocab), 1) == token
    target = jnp.sum(jnp.where(hit, x, 0.0), axis=1, keepdims=True)
    peak = jnp.max(x, axis=1, keepdims=True)
    mass = jnp.sum(jnp.exp(x - peak), axis=1, keepdims=True)
    ratio = target - (peak + jnp.log(mass))
    mine_row = jnp.sum(jnp.where(mine, ratio - logp_ref[...], 0.0), axis=0, keepdims=True)
    out_ref[...] = jnp.broadcast_to(mine_row[None], out_ref.shape)


def body(queries, keys, values, readout, token_ids, stored_logp, span_order):
    rows = queries.shape[0]
    ids = jnp.stack([lax.axis_index("ctx"), lax.axis_index("tp")]).astype(jnp.int32)
    q_all, bias = prep(ids, span_order, queries)

    kv = lax.all_to_all(pack(keys, values), "ctx", 0, 0, axis_index_groups=Y_GROUPS, tiled=True)
    a, b = swap_z(kv, 0), swap_z(kv, 1)
    start = Y * rows
    state = attend(q_all, bias, [kv], 0)
    for step in range(1, Z // 2):
        now = [a, b]
        if step == Z // 2 - 1:
            a, b = a[: Y // 2], b[Y // 2 :]
        a, b = swap_z(a, step % 2), swap_z(b, 1 - step % 2)
        state = attend(q_all, bias, now, start, state)
        start += 2 * Y * rows
    attended, parts = attend(q_all, bias, [a, b], start, state, readout)

    parts = lax.all_to_all(parts, "tp", 0, 0, tiled=True)
    args = [parts, token_ids.reshape(1, rows), stored_logp.reshape(1, rows)]
    ratio = pl.pallas_call(
        ratio_kernel,
        out_shape=jax.ShapeDtypeStruct((TP, 1, rows), jnp.float32),
        in_specs=[SMEM] + [VMEM] * len(args),
        out_specs=VMEM,
        name="ratio",
    )(ids, *args)
    ratio = lax.all_to_all(ratio, "tp", 0, 0, tiled=True)
    return attended, jnp.sum(ratio, axis=(0, 1))


def solution(mesh):
    return jax.shard_map(
        body,
        mesh=mesh,
        in_specs=(
            P(("dp", "ctx"), "tp"),
            P(("dp", "ctx"), "tp"),
            P(("dp", "ctx"), "tp"),
            P("tp", None),
            P(("dp", "ctx")),
            P(("dp", "ctx")),
            P("dp"),
        ),
        out_specs=(P(("dp", "ctx"), "tp"), P(("dp", "ctx"))),
        check_vma=False,
    )
```

time: 290 us -> 91.6 us (0.32)
  the two profiles are of different devices: /device:TPU:16 before, /device:TPU:2 now
where the time goes in v1:
time: 91.6 us; the launch traced here: 90.9 us
  starting transfers between devices  36.8 us (40%)
  blocking collectives  19.1 us (21%)
  waiting for transfers between devices  18.5 us (20%)
  Pallas kernels  13.6 us (15%)
  local copies, waits for them, and re-layouts  1.63 us (2%)
    ppermute x8, starting transfers between devices, swap_z(): return lax.ppermute(x, 'ctx', pairs)  29.7 us
    all_to_all x1, blocking collectives, body(): parts = lax.all_to_all(parts, 'tp', 0, 0, tiled=True)  10.7 us
    all_to_all x1, waiting for transfers between devices, body(): lax.all_to_all(pack(keys, values), 'ctx', 0, 0, axis_index_groups=Y_GROUP...  10.3 us
    pallas_call x5, Pallas kernels, attend(): pl.pallas_call(functools.partial(attend_kernel, start, len(kvs), first, l...  9.1 us
    all_to_all x1, blocking collectives, body(): ratio = lax.all_to_all(ratio, 'tp', 0, 0, tiled=True)  8.42 us
    ppermute x8, waiting for transfers between devices, swap_z(): return lax.ppermute(x, 'ctx', pairs)  8.1 us
    all_to_all x1, starting transfers between devices, body(): lax.all_to_all(pack(keys, values), 'ctx', 0, 0, axis_index_groups=Y_GROUP...  7.11 us
    pallas_call x1, Pallas kernels, body(): pl.pallas_call(ratio_kernel, out_shape=jax.ShapeDtypeStruct((TP, 1, rows)...  1.84 us
  transfers between devices with their start and end apart: 9, of which 5 were waited for; matrix products, arithmetic and copies ran while one was open for 0% of the time, Pallas kernels for 9%

profile of v1, /device:TPU:2, one launch (start us, length us, event | category | flops | bytes accessed | tf_op | source)
XLA Modules:
  0.0 90.9 jit_solution(16871779847031946115)
XLA Ops:
  0.6 1.7 %pack.1 = bf16[4,128,256]{2,1,0:T(8,128)(2,1)} custom-call(bf16[128,128]{1,0:T(8,128)(2,1)} %k_ref.1, bf16[128,128]{1,0:T(8,128)(2,1)} %v_ref.1), custom_call_target="tpu_custom_call" | custom-call | tf_op jit(solution)/shard_map/pack/pallas_call | solution.py:60
  2.3 7.1 %all-to-all-start = ((bf16[4,128,256]{2,1,0:T(8,128)(2,1)}), bf16[4,128,256]{2,1,0:T(8,128)(2,1)S(1)}, u32[]{:S(2)}, u32[]{:S(2)}) async-start(bf16[4,128,256]{2,1,0:T(8,128)(2,1)} %pack.1), calls=%async_computation | async-start | bytes 524288 | tf_op jit(solution)/shard_map/all_to_all | solution.py:216
  9.5 10.3 %all-to-all-done.refs_0_ = bf16[4,128,256]{2,1,0:T(8,128)(2,1)S(1)} async-done(((bf16[4,128,256]{2,1,0:T(8,128)(2,1)}), bf16[4,128,256]{2,1,0:T(8,128)(2,1)S(1)}, u32[]{:S(2)}, u32[]{:S(2)}) %all-to-all-start) | async-done | bytes 262176 | tf_op jit(solution)/shard_map/all_to_all | solution.py:216
  19.9 4.3 %collective-permute-start = (bf16[4,128,256]{2,1,0:T(8,128)(2,1)S(1)}, bf16[4,128,256]{2,1,0:T(8,128)(2,1)S(1)}, u32[]{:S(2)}, u32[]{:S(2)}) collective-permute-start(bf16[4,128,256]{2,1,0:T(8,128)(2,1)S(1)} %all-to-all-done.refs_0_), channel_id=1, source_target_pairs={{0,16},{4,20},{8,24},{12,28},{16,0},{20,4},{24,8},{28,12},{32,48},... | collective-permute-start | bytes 786440 | tf_op jit(solution)/shard_map/ppermute | solution.py:28
  24.2 9.1 %collective-permute-start.4 = (bf16[4,128,256]{2,1,0:T(8,128)(2,1)S(1)}, bf16[4,128,256]{2,1,0:T(8,128)(2,1)S(1)}, u32[]{:S(2)}, u32[]{:S(2)}) collective-permute-start(bf16[4,128,256]{2,1,0:T(8,128)(2,1)S(1)} %all-to-all-done.refs_0_), channel_id=1, source_target_pairs={{0,112},{4,116},{8,120},{12,124},{16,32},{20,36},{24,40},{28,44},{... | collective-permute-start | bytes 786440 | tf_op jit(solution)/shard_map/ppermute | solution.py:28
  33.3 0.9 %copy-done.2 = bf16[128,1024]{1,0:T(8,128)(2,1)S(1)} copy-done((bf16[128,1024]{1,0:T(8,128)(2,1)S(1)}, bf16[128,1024]{1,0:T(8,128)(2,1)}, u32[]{:S(2)}) %copy-start.2) | copy-done | bytes 262168
  34.9 0.9 %prep.1 = (bf16[1024,256]{1,0:T(8,128)(2,1)S(1)}, bf16[4096,128]{1,0:T(8,128)(2,1)S(1)}) custom-call(s32[2]{0:T(128)S(1)} %pad_add_fusion.ids, s32[64]{0:T(128)S(1)} %copy-done.3, bf16[128,1024]{1,0:T(8,128)(2,1)S(1)} %copy-done.2), custom_call_target="tpu_custom_call" | custom-call | flops 2000000000 | bytes 2097152 | tf_op jit(solution)/shard_map/prep/pallas_call | solution.py:105
  35.8 1.0 %attend.4 = (f32[1024,256]{1,0:T(8,128)S(1)}, f32[1024,128]{1,0:T(8,128)S(1)}) custom-call(bf16[1024,256]{1,0:T(8,128)(2,1)S(1)} %get-tuple-element.14.q_all, bf16[4096,128]{1,0:T(8,128)(2,1)S(1)} %get-tuple-element.15.bias_ref, bf16[4,128,256]{2,1,0:T(8,128)(2,1)S(1)} %all-to-all-done.refs_0_), custom_call_target="tpu_custom_call" | custom-call | flops 2147483648 | bytes 4194304 | tf_op jit(solution)/shard_map/attend/pallas_call | solution.py:176
  36.9 2.2 %collective-permute-start.1 = (bf16[4,128,256]{2,1,0:T(8,128)(2,1)S(1)}, bf16[4,128,256]{2,1,0:T(8,128)(2,1)S(1)}, u32[]{:S(2)}, u32[]{:S(2)}) collective-permute-start(bf16[4,128,256]{2,1,0:T(8,128)(2,1)S(1)} %collective-permute-done.refs_0_), channel_id=1, source_target_pairs={{0,112},{4,116},{8,120},{12,124},{16,32},{20,36},{24,40},{28,44},{... | collective-permute-start | bytes 786440 | tf_op jit(solution)/shard_map/ppermute | solution.py:28
  39.1 1.9 %collective-permute-start.5 = (bf16[4,128,256]{2,1,0:T(8,128)(2,1)S(1)}, bf16[4,128,256]{2,1,0:T(8,128)(2,1)S(1)}, u32[]{:S(2)}, u32[]{:S(2)}) collective-permute-start(bf16[4,128,256]{2,1,0:T(8,128)(2,1)S(1)} %collective-permute-done.4.refs_1_), channel_id=1, source_target_pairs={{0,16},{4,20},{8,24},{12,28},{16,0},{20,4},{24,8},{28,12},{32,48},... | collective-permute-start | bytes 786440 | tf_op jit(solution)/shard_map/ppermute | solution.py:28
  41.0 2.0 %attend.5 = (f32[1024,256]{1,0:T(8,128)S(1)}, f32[1024,128]{1,0:T(8,128)S(1)}) custom-call(bf16[1024,256]{1,0:T(8,128)(2,1)S(1)} %get-tuple-element.14.q_all, bf16[4096,128]{1,0:T(8,128)(2,1)S(1)} %get-tuple-element.15.bias_ref, bf16[4,128,256]{2,1,0:T(8,128)(2,1)S(1)} %collective-permute-done.refs_0_, ...), custom_call_target="tpu_custom_call" | custom-call | flops 4294967296 | bytes 4194304 | tf_op jit(solution)/shard_map/attend/pallas_call | solution.py:176
  43.0 3.3 %collective-permute-done.1.refs_0_ = bf16[4,128,256]{2,1,0:T(8,128)(2,1)S(1)} collective-permute-done((bf16[4,128,256]{2,1,0:T(8,128)(2,1)S(1)}, bf16[4,128,256]{2,1,0:T(8,128)(2,1)S(1)}, u32[]{:S(2)}, u32[]{:S(2)}) %collective-permute-start.1) | collective-permute-done | bytes 262176 | tf_op jit(solution)/shard_map/ppermute | solution.py:28
  46.3 1.9 %collective-permute-start.2 = (bf16[4,128,256]{2,1,0:T(8,128)(2,1)S(1)}, bf16[4,128,256]{2,1,0:T(8,128)(2,1)S(1)}, u32[]{:S(2)}, u32[]{:S(2)}) collective-permute-start(bf16[4,128,256]{2,1,0:T(8,128)(2,1)S(1)} %collective-permute-done.1.refs_0_), channel_id=1, source_target_pairs={{0,16},{4,20},{8,24},{12,28},{16,0},{20,4},{24,8},{28,12},{32,48},... | collective-permute-start | bytes 786440 | tf_op jit(solution)/shard_map/ppermute | solution.py:28
  48.3 6.4 %collective-permute-start.6 = (bf16[4,128,256]{2,1,0:T(8,128)(2,1)S(1)}, bf16[4,128,256]{2,1,0:T(8,128)(2,1)S(1)}, u32[]{:S(2)}, u32[]{:S(2)}) collective-permute-start(bf16[4,128,256]{2,1,0:T(8,128)(2,1)S(1)} %collective-permute-done.5.refs_1_), channel_id=1, source_target_pairs={{0,112},{4,116},{8,120},{12,124},{16,32},{20,36},{24,40},{28,44},{... | collective-permute-start | bytes 786440 | tf_op jit(solution)/shard_map/ppermute | solution.py:28
  54.7 2.0 %attend.6 = (f32[1024,256]{1,0:T(8,128)S(1)}, f32[1024,128]{1,0:T(8,128)S(1)}) custom-call(bf16[1024,256]{1,0:T(8,128)(2,1)S(1)} %get-tuple-element.14.q_all, bf16[4096,128]{1,0:T(8,128)(2,1)S(1)} %get-tuple-element.15.bias_ref, bf16[4,128,256]{2,1,0:T(8,128)(2,1)S(1)} %collective-permute-done.1.refs_0_, ...), custom_call_target="tpu_custom_call" | custom-call | flops 4294967296 | bytes 4194304 | tf_op jit(solution)/shard_map/attend/pallas_call | solution.py:176
  56.7 1.9 %collective-permute-start.3 = (bf16[2,128,256]{2,1,0:T(8,128)(2,1)S(1)}, bf16[2,128,256]{2,1,0:T(8,128)(2,1)S(1)}, u32[]{:S(2)}, u32[]{:S(2)}) collective-permute-start(bf16[2,128,256]{2,1,0:T(8,128)(2,1)S(1)} %slice.8), channel_id=1, source_target_pairs={{0,112},{4,116},{8,120},{12,124},{16,32},{20,36},{24,40},{28,44},{... | collective-permute-start | bytes 393224 | tf_op jit(solution)/shard_map/ppermute | solution.py:28
  58.7 1.8 %collective-permute-done.6.refs_1_ = bf16[4,128,256]{2,1,0:T(8,128)(2,1)S(1)} collective-permute-done((bf16[4,128,256]{2,1,0:T(8,128)(2,1)S(1)}, bf16[4,128,256]{2,1,0:T(8,128)(2,1)S(1)}, u32[]{:S(2)}, u32[]{:S(2)}) %collective-permute-start.6) | collective-permute-done | bytes 262176 | tf_op jit(solution)/shard_map/ppermute | solution.py:28
  60.5 1.9 %collective-permute-start.7 = (bf16[2,128,256]{2,1,0:T(8,128)(2,1)S(1)}, bf16[2,128,256]{2,1,0:T(8,128)(2,1)S(1)}, u32[]{:S(2)}, u32[]{:S(2)}) collective-permute-start(bf16[2,128,256]{2,1,0:T(8,128)(2,1)S(1)} %slice.9), channel_id=1, source_target_pairs={{0,16},{4,20},{8,24},{12,28},{16,0},{20,4},{24,8},{28,12},{32,48},... | collective-permute-start | bytes 393224 | tf_op jit(solution)/shard_map/ppermute | solution.py:28
  62.4 2.0 %attend.7 = (f32[1024,256]{1,0:T(8,128)S(1)}, f32[1024,128]{1,0:T(8,128)S(1)}) custom-call(bf16[1024,256]{1,0:T(8,128)(2,1)S(1)} %get-tuple-element.14.q_all, bf16[4096,128]{1,0:T(8,128)(2,1)S(1)} %get-tuple-element.15.bias_ref, bf16[4,128,256]{2,1,0:T(8,128)(2,1)S(1)} %collective-permute-done.2.refs_0_, ...), custom_call_target="tpu_custom_call" | custom-call | flops 4294967296 | bytes 4194304 | tf_op jit(solution)/shard_map/attend/pallas_call | solution.py:176
  64.8 2.5 %collective-permute-done.7.refs_1_ = bf16[2,128,256]{2,1,0:T(8,128)(2,1)S(1)} collective-permute-done((bf16[2,128,256]{2,1,0:T(8,128)(2,1)S(1)}, bf16[2,128,256]{2,1,0:T(8,128)(2,1)S(1)}, u32[]{:S(2)}, u32[]{:S(2)}) %collective-permute-start.7) | collective-permute-done | bytes 131104 | tf_op jit(solution)/shard_map/ppermute | solution.py:28
  67.3 2.2 %attend_last.1 = (bf16[128,1024]{1,0:T(8,128)(2,1)}, bf16[4,32,1536]{2,1,0:T(8,128)(2,1)S(1)}) custom-call(bf16[1024,256]{1,0:T(8,128)(2,1)S(1)} %get-tuple-element.14.q_all, bf16[4096,128]{1,0:T(8,128)(2,1)S(1)} %get-tuple-element.15.bias_ref, bf16[2,128,256]{2,1,0:T(8,128)(2,1)S(1)} %collective-permute-done.3.refs_0_, ...), custom_call_target="tpu_custom_call" | custom-call | flops 2147483648 | bytes 4194304 | tf_op jit(solution)/shard_map/attend_last/pallas_call | solution.py:176
  69.5 10.7 %all_to_all.15.part_ref = bf16[4,32,1536]{2,1,0:T(8,128)(2,1)} all-to-all(bf16[4,32,1536]{2,1,0:T(8,128)(2,1)S(1)} %get-tuple-element.25), channel_id=1, replica_groups=mesh['dp'=4,'ctx'=32,'tp'=4] {'tp'}, dimensions={0} | all-to-all | bytes 786432 | tf_op jit(solution)/shard_map/all_to_all | solution.py:229
  80.1 1.8 %ratio.1 = f32[4,1,128]{2,1,0:T(1,128)} custom-call(s32[2]{0:T(128)} %copy-done, bf16[4,32,1536]{2,1,0:T(8,128)(2,1)} %all_to_all.15.part_ref, s32[1,128]{1,0:T(1,128)} %bitcast.4, f32[1,128]{1,0:T(1,128)} %bitcast.5), custom_call_target="tpu_custom_call" | custom-call | tf_op jit(solution)/shard_map/ratio/pallas_call | solution.py:231
  82.0 8.4 %all_to_all.16 = f32[4,1,128]{2,1,0:T(1,128)S(1)} all-to-all(f32[4,1,128]{2,1,0:T(1,128)} %ratio.1), channel_id=1, replica_groups=mesh['dp'=4,'ctx'=32,'tp'=4] {'tp'}, dimensions={0} | all-to-all | bytes 4096 | tf_op jit(solution)/shard_map/all_to_all | solution.py:238
  (16 shorter events, 1.7 us)
Async XLA Ops:
  2.3 17.5 %all-to-all-start = ((bf16[4,128,256]{2,1,0:T(8,128)(2,1)}), bf16[4,128,256]{2,1,0:T(8,128)(2,1)S(1)}, u32[]{:S(2)}, u32[]{:S(2)}) async-start(bf16[4,128,256]{2,1,0:T(8,128)(2,1)} %pack.1), calls=%async_computation | async-start | bytes 524288 | tf_op jit(solution)/shard_map/all_to_all | solution.py:216
  9.5 26.3 %copy-start = (s32[2]{0:T(128)}, s32[2]{0:T(128)S(1)}, u32[]{:S(2)}) copy-start(s32[2]{0:T(128)S(1)} %pad_add_fusion.ids) | copy-start | bytes 28
  19.9 17.0 %collective-permute-start = (bf16[4,128,256]{2,1,0:T(8,128)(2,1)S(1)}, bf16[4,128,256]{2,1,0:T(8,128)(2,1)S(1)}, u32[]{:S(2)}, u32[]{:S(2)}) collective-permute-start(bf16[4,128,256]{2,1,0:T(8,128)(2,1)S(1)} %all-to-all-done.refs_0_), channel_id=1, source_target_pairs={{0,16},{4,20},{8,24},{12,28},{16,0},{20,4},{24,8},{28,12},{32,48},... | collective-permute-start | bytes 786440 | tf_op jit(solution)/shard_map/ppermute | solution.py:28
  24.2 14.9 %collective-permute-start.4 = (bf16[4,128,256]{2,1,0:T(8,128)(2,1)S(1)}, bf16[4,128,256]{2,1,0:T(8,128)(2,1)S(1)}, u32[]{:S(2)}, u32[]{:S(2)}) collective-permute-start(bf16[4,128,256]{2,1,0:T(8,128)(2,1)S(1)} %all-to-all-done.refs_0_), channel_id=1, source_target_pairs={{0,112},{4,116},{8,120},{12,124},{16,32},{20,36},{24,40},{28,44},{... | collective-permute-start | bytes 786440 | tf_op jit(solution)/shard_map/ppermute | solution.py:28
  33.3 1.0 %copy-start.2 = (bf16[128,1024]{1,0:T(8,128)(2,1)S(1)}, bf16[128,1024]{1,0:T(8,128)(2,1)}, u32[]{:S(2)}) copy-start(bf16[128,1024]{1,0:T(8,128)(2,1)} %q_ref.1) | copy-start | bytes 786436
  34.2 0.7 copy-start.3
  36.9 9.5 %collective-permute-start.1 = (bf16[4,128,256]{2,1,0:T(8,128)(2,1)S(1)}, bf16[4,128,256]{2,1,0:T(8,128)(2,1)S(1)}, u32[]{:S(2)}, u32[]{:S(2)}) collective-permute-start(bf16[4,128,256]{2,1,0:T(8,128)(2,1)S(1)} %collective-permute-done.refs_0_), channel_id=1, source_target_pairs={{0,112},{4,116},{8,120},{12,124},{16,32},{20,36},{24,40},{28,44},{... | collective-permute-start | bytes 786440 | tf_op jit(solution)/shard_map/ppermute | solution.py:28
  39.1 9.2 %collective-permute-start.5 = (bf16[4,128,256]{2,1,0:T(8,128)(2,1)S(1)}, bf16[4,128,256]{2,1,0:T(8,128)(2,1)S(1)}, u32[]{:S(2)}, u32[]{:S(2)}) collective-permute-start(bf16[4,128,256]{2,1,0:T(8,128)(2,1)S(1)} %collective-permute-done.4.refs_1_), channel_id=1, source_target_pairs={{0,16},{4,20},{8,24},{12,28},{16,0},{20,4},{24,8},{28,12},{32,48},... | collective-permute-start | bytes 786440 | tf_op jit(solution)/shard_map/ppermute | solution.py:28
  46.3 10.4 %collective-permute-start.2 = (bf16[4,128,256]{2,1,0:T(8,128)(2,1)S(1)}, bf16[4,128,256]{2,1,0:T(8,128)(2,1)S(1)}, u32[]{:S(2)}, u32[]{:S(2)}) collective-permute-start(bf16[4,128,256]{2,1,0:T(8,128)(2,1)S(1)} %collective-permute-done.1.refs_0_), channel_id=1, source_target_pairs={{0,16},{4,20},{8,24},{12,28},{16,0},{20,4},{24,8},{28,12},{32,48},... | collective-permute-start | bytes 786440 | tf_op jit(solution)/shard_map/ppermute | solution.py:28
  48.3 12.2 %collective-permute-start.6 = (bf16[4,128,256]{2,1,0:T(8,128)(2,1)S(1)}, bf16[4,128,256]{2,1,0:T(8,128)(2,1)S(1)}, u32[]{:S(2)}, u32[]{:S(2)}) collective-permute-start(bf16[4,128,256]{2,1,0:T(8,128)(2,1)S(1)} %collective-permute-done.5.refs_1_), channel_id=1, source_target_pairs={{0,112},{4,116},{8,120},{12,124},{16,32},{20,36},{24,40},{28,44},{... | collective-permute-start | bytes 786440 | tf_op jit(solution)/shard_map/ppermute | solution.py:28
  56.7 8.1 %collective-permute-start.3 = (bf16[2,128,256]{2,1,0:T(8,128)(2,1)S(1)}, bf16[2,128,256]{2,1,0:T(8,128)(2,1)S(1)}, u32[]{:S(2)}, u32[]{:S(2)}) collective-permute-start(bf16[2,128,256]{2,1,0:T(8,128)(2,1)S(1)} %slice.8), channel_id=1, source_target_pairs={{0,112},{4,116},{8,120},{12,124},{16,32},{20,36},{24,40},{28,44},{... | collective-permute-start | bytes 393224 | tf_op jit(solution)/shard_map/ppermute | solution.py:28
  60.5 6.9 %collective-permute-start.7 = (bf16[2,128,256]{2,1,0:T(8,128)(2,1)S(1)}, bf16[2,128,256]{2,1,0:T(8,128)(2,1)S(1)}, u32[]{:S(2)}, u32[]{:S(2)}) collective-permute-start(bf16[2,128,256]{2,1,0:T(8,128)(2,1)S(1)} %slice.9), channel_id=1, source_target_pairs={{0,16},{4,20},{8,24},{12,28},{16,0},{20,4},{24,8},{28,12},{32,48},... | collective-permute-start | bytes 393224 | tf_op jit(solution)/shard_map/ppermute | solution.py:28
  62.4 4.9 %copy-start.1 = (bf16[1024,1536]{1,0:T(8,128)(2,1)S(1)}, bf16[1024,1536]{1,0:T(8,128)(2,1)}, u32[]{:S(2)}) copy-start(bf16[1024,1536]{1,0:T(8,128)(2,1)} %refs_4_.1) | copy-start | bytes 9437188

commit v2 on v1

--- a/solution.py
+++ b/solution.py
@@ -46,14 +46,16 @@
 
 
 def pack_kernel(k_ref, v_ref, out_ref, sems):
-    copies = []
-    for j in range(Y):
-        copies.append(pltpu.make_async_copy(k_ref, out_ref.at[j, :, pl.ds(0, HEAD)], sems.at[2 * j]))
-        copies.append(pltpu.make_async_copy(v_ref, out_ref.at[j, :, pl.ds(HEAD, HEAD)], sems.at[2 * j + 1]))
+    copies = [
+        pltpu.make_async_copy(k_ref, out_ref.at[0, :, pl.ds(0, HEAD)], sems.at[0]),
+        pltpu.make_async_copy(v_ref, out_ref.at[0, :, pl.ds(HEAD, HEAD)], sems.at[1]),
+    ]
     for copy in copies:
         copy.start()
     for copy in copies:
         copy.wait()
+    for j in range(1, Y):
+        out_ref[j] = out_ref[0]
 
 
 def pack(keys, values):
@@ -62,7 +64,7 @@
         out_shape=jax.ShapeDtypeStruct((Y, keys.shape[0], 2 * HEAD), keys.dtype),
         in_specs=[HBM] * 2,
         out_specs=VMEM,
-        scratch_shapes=[pltpu.SemaphoreType.DMA((2 * Y,))],
+        scratch_shapes=[pltpu.SemaphoreType.DMA((2,))],
         name="pack",
     )(keys, values)
 
@@ -204,8 +206,7 @@
     peak = jnp.max(x, axis=1, keepdims=True)
     mass = jnp.sum(jnp.exp(x - peak), axis=1, keepdims=True)
     ratio = target - (peak + jnp.log(mass))
-    mine_row = jnp.sum(jnp.where(mine, ratio - logp_ref[...], 0.0), axis=0, keepdims=True)
-    out_ref[...] = jnp.broadcast_to(mine_row[None], out_ref.shape)
+    out_ref[...] = jnp.sum(jnp.where(mine, ratio - logp_ref[...], 0.0), axis=0, keepdims=True)
 
 
 def body(queries, keys, values, readout, token_ids, stored_logp, span_order):
@@ -214,29 +215,34 @@
     q_all, bias = prep(ids, span_order, queries)
 
     kv = lax.all_to_all(pack(keys, values), "ctx", 0, 0, axis_index_groups=Y_GROUPS, tiled=True)
+    kv, q_all, bias = lax.optimization_barrier((kv, q_all, bias))
     a, b = swap_z(kv, 0), swap_z(kv, 1)
     start = Y * rows
     state = attend(q_all, bias, [kv], 0)
-    for step in range(1, Z // 2):
+    now = [a, b]
+    a, b = swap_z(a, 1), swap_z(b, 0)
+    for step in range(2, Z // 2 + 1):
+        last = step == Z // 2
+        state = attend(q_all, bias, now, start, state)
+        start += 2 * Y * rows
+        if last:
+            break
         now = [a, b]
         if step == Z // 2 - 1:
             a, b = a[: Y // 2], b[Y // 2 :]
         a, b = swap_z(a, step % 2), swap_z(b, 1 - step % 2)
-        state = attend(q_all, bias, now, start, state)
-        start += 2 * Y * rows
     attended, parts = attend(q_all, bias, [a, b], start, state, readout)
 
     parts = lax.all_to_all(parts, "tp", 0, 0, tiled=True)
     args = [parts, token_ids.reshape(1, rows), stored_logp.reshape(1, rows)]
     ratio = pl.pallas_call(
         ratio_kernel,
-        out_shape=jax.ShapeDtypeStruct((TP, 1, rows), jnp.float32),
+        out_shape=jax.ShapeDtypeStruct((1, rows), jnp.float32),
         in_specs=[SMEM] + [VMEM] * len(args),
         out_specs=VMEM,
         name="ratio",
     )(ids, *args)
-    ratio = lax.all_to_all(ratio, "tp", 0, 0, tiled=True)
-    return attended, jnp.sum(ratio, axis=(0, 1))
+    return attended, lax.psum(ratio.reshape(rows), "tp")
 
 
 def solution(mesh):

time: 91.6 us -> 92.1 us (level)
  starting transfers between devices: 36.8 us -> 39.7 us
  waiting for transfers between devices: 18.5 us -> 15.6 us
  blocking collectives: 19.1 us -> 20.5 us
    psum x0 -> x1, blocking collectives: none -> 9.79 us  [body(): return (attended, lax.psum(ratio.reshape(rows), 'tp'))]
    all_to_all x1 -> x0, blocking collectives: 8.42 us -> none  [body(): ratio = lax.all_to_all(ratio, 'tp', 0, 0, tiled=True)]
    ppermute x8, starting transfers between devices: 29.7 us -> 32.6 us  [swap_z(): return lax.ppermute(x, 'ctx', pairs)]
    all_to_all x1, waiting for transfers between devices: 10.3 us -> 7.81 us  [body(): lax.all_to_all(pack(keys, values), 'ctx', 0, 0, axis_index_groups=Y_GROUP...]
  transfers between devices with their start and end apart: 9 -> 9, of which waited for: 5 -> 6; matrix products, arithmetic and copies ran while one was open for 0% -> 0% of each run, Pallas kernels for 9% -> 9%
where the time goes in v2:
time: 92.1 us; the launch traced here: 91.5 us
  starting transfers between devices  39.7 us (43%)
  blocking collectives  20.5 us (22%)
  waiting for transfers between devices  15.6 us (17%)
  Pallas kernels  13.3 us (14%)
  local copies, waits for them, and re-layouts  1.63 us (2%)
    ppermute x8, starting transfers between devices, swap_z(): return lax.ppermute(x, 'ctx', pairs)  32.6 us
    all_to_all x1, blocking collectives, body(): parts = lax.all_to_all(parts, 'tp', 0, 0, tiled=True)  10.7 us
    psum x1, blocking collectives, body(): return (attended, lax.psum(ratio.reshape(rows), 'tp'))  9.79 us
    pallas_call x5, Pallas kernels, attend(): pl.pallas_call(functools.partial(attend_kernel, start, len(kvs), first, l...  9.1 us
    all_to_all x1, waiting for transfers between devices, body(): lax.all_to_all(pack(keys, values), 'ctx', 0, 0, axis_index_groups=Y_GROUP...  7.81 us
    ppermute x8, waiting for transfers between devices, swap_z(): return lax.ppermute(x, 'ctx', pairs)  7.76 us
    all_to_all x1, starting transfers between devices, body(): lax.all_to_all(pack(keys, values), 'ctx', 0, 0, axis_index_groups=Y_GROUP...  7.11 us
  transfers between devices with their start and end apart: 9, of which 6 were waited for; matrix products, arithmetic and copies ran while one was open for 0% of the time, Pallas kernels for 9%

profile of v2, /device:TPU:2, one launch (start us, length us, event | category | flops | bytes accessed | tf_op | source)
XLA Modules:
  0.0 91.5 jit_solution(8334003191927120745)
XLA Ops:
  0.6 1.5 %pack.1 = bf16[4,128,256]{2,1,0:T(8,128)(2,1)} custom-call(bf16[128,128]{1,0:T(8,128)(2,1)} %k_ref.1, bf16[128,128]{1,0:T(8,128)(2,1)} %v_ref.1), custom_call_target="tpu_custom_call" | custom-call | tf_op jit(solution)/shard_map/pack/pallas_call | solution.py:62
  2.1 7.1 %all-to-all-start = ((bf16[4,128,256]{2,1,0:T(8,128)(2,1)}), bf16[4,128,256]{2,1,0:T(8,128)(2,1)S(1)}, u32[]{:S(2)}, u32[]{:S(2)}) async-start(bf16[4,128,256]{2,1,0:T(8,128)(2,1)} %pack.1), calls=%async_computation | async-start | bytes 524288 | tf_op jit(solution)/shard_map/all_to_all | solution.py:217
  9.3 0.9 %copy-done.2 = bf16[128,1024]{1,0:T(8,128)(2,1)S(1)} copy-done((bf16[128,1024]{1,0:T(8,128)(2,1)S(1)}, bf16[128,1024]{1,0:T(8,128)(2,1)}, u32[]{:S(2)}) %copy-start.2) | copy-done | bytes 262168
  11.9 7.8 %all-to-all-done.refs_0_ = bf16[4,128,256]{2,1,0:T(8,128)(2,1)S(1)} async-done(((bf16[4,128,256]{2,1,0:T(8,128)(2,1)}), bf16[4,128,256]{2,1,0:T(8,128)(2,1)S(1)}, u32[]{:S(2)}, u32[]{:S(2)}) %all-to-all-start) | async-done | bytes 262176 | tf_op jit(solution)/shard_map/all_to_all | solution.py:217
  19.7 4.3 %collective-permute-start = (bf16[4,128,256]{2,1,0:T(8,128)(2,1)S(1)}, bf16[4,128,256]{2,1,0:T(8,128)(2,1)S(1)}, u32[]{:S(2)}, u32[]{:S(2)}) collective-permute-start(bf16[4,128,256]{2,1,0:T(8,128)(2,1)S(1)} %all-to-all-done.refs_0_), channel_id=1, source_target_pairs={{0,16},{4,20},{8,24},{12,28},{16,0},{20,4},{24,8},{28,12},{32,48},... | collective-permute-start | bytes 786440 | tf_op jit(solution)/shard_map/ppermute | solution.py:28
  24.0 9.1 %collective-permute-start.4 = (bf16[4,128,256]{2,1,0:T(8,128)(2,1)S(1)}, bf16[4,128,256]{2,1,0:T(8,128)(2,1)S(1)}, u32[]{:S(2)}, u32[]{:S(2)}) collective-permute-start(bf16[4,128,256]{2,1,0:T(8,128)(2,1)S(1)} %all-to-all-done.refs_0_), channel_id=1, source_target_pairs={{0,112},{4,116},{8,120},{12,124},{16,32},{20,36},{24,40},{28,44},{... | collective-permute-start | bytes 786440 | tf_op jit(solution)/shard_map/ppermute | solution.py:28
  33.1 1.0 %attend.4 = (f32[1024,256]{1,0:T(8,128)S(1)}, f32[1024,128]{1,0:T(8,128)S(1)}) custom-call(bf16[1024,256]{1,0:T(8,128)(2,1)S(1)} %get-tuple-element.19.q_all, bf16[4096,128]{1,0:T(8,128)(2,1)S(1)} %get-tuple-element.20.bias_ref, bf16[4,128,256]{2,1,0:T(8,128)(2,1)S(1)} %all-to-all-done.refs_0_), custom_call_target="tpu_custom_call" | custom-call | flops 2147483648 | bytes 4194304 | tf_op jit(solution)/shard_map/attend/pallas_call | solution.py:178
  34.1 4.8 %collective-permute-start.1 = (bf16[4,128,256]{2,1,0:T(8,128)(2,1)S(1)}, bf16[4,128,256]{2,1,0:T(8,128)(2,1)S(1)}, u32[]{:S(2)}, u32[]{:S(2)}) collective-permute-start(bf16[4,128,256]{2,1,0:T(8,128)(2,1)S(1)} %collective-permute-done.refs_0_), channel_id=1, source_target_pairs={{0,112},{4,116},{8,120},{12,124},{16,32},{20,36},{24,40},{28,44},{... | collective-permute-start | bytes 786440 | tf_op jit(solution)/shard_map/ppermute | solution.py:28
  38.9 1.9 %collective-permute-start.5 = (bf16[4,128,256]{2,1,0:T(8,128)(2,1)S(1)}, bf16[4,128,256]{2,1,0:T(8,128)(2,1)S(1)}, u32[]{:S(2)}, u32[]{:S(2)}) collective-permute-start(bf16[4,128,256]{2,1,0:T(8,128)(2,1)S(1)} %collective-permute-done.4.refs_1_), channel_id=1, source_target_pairs={{0,16},{4,20},{8,24},{12,28},{16,0},{20,4},{24,8},{28,12},{32,48},... | collective-permute-start | bytes 786440 | tf_op jit(solution)/shard_map/ppermute | solution.py:28
  40.8 2.0 %attend.5 = (f32[1024,256]{1,0:T(8,128)S(1)}, f32[1024,128]{1,0:T(8,128)S(1)}) custom-call(bf16[1024,256]{1,0:T(8,128)(2,1)S(1)} %get-tuple-element.19.q_all, bf16[4096,128]{1,0:T(8,128)(2,1)S(1)} %get-tuple-element.20.bias_ref, bf16[4,128,256]{2,1,0:T(8,128)(2,1)S(1)} %collective-permute-done.refs_0_, ...), custom_call_target="tpu_custom_call" | custom-call | flops 4294967296 | bytes 4194304 | tf_op jit(solution)/shard_map/attend/pallas_call | solution.py:178
  43.6 3.1 %collective-permute-start.2 = (bf16[4,128,256]{2,1,0:T(8,128)(2,1)S(1)}, bf16[4,128,256]{2,1,0:T(8,128)(2,1)S(1)}, u32[]{:S(2)}, u32[]{:S(2)}) collective-permute-start(bf16[4,128,256]{2,1,0:T(8,128)(2,1)S(1)} %collective-permute-done.1.refs_0_), channel_id=1, source_target_pairs={{0,16},{4,20},{8,24},{12,28},{16,0},{20,4},{24,8},{28,12},{32,48},... | collective-permute-start | bytes 786440 | tf_op jit(solution)/shard_map/ppermute | solution.py:28
  46.7 3.0 %collective-permute-done.5.refs_1_ = bf16[4,128,256]{2,1,0:T(8,128)(2,1)S(1)} collective-permute-done((bf16[4,128,256]{2,1,0:T(8,128)(2,1)S(1)}, bf16[4,128,256]{2,1,0:T(8,128)(2,1)S(1)}, u32[]{:S(2)}, u32[]{:S(2)}) %collective-permute-start.5) | collective-permute-done | bytes 262176 | tf_op jit(solution)/shard_map/ppermute | solution.py:28
  49.8 5.5 %collective-permute-start.6 = (bf16[4,128,256]{2,1,0:T(8,128)(2,1)S(1)}, bf16[4,128,256]{2,1,0:T(8,128)(2,1)S(1)}, u32[]{:S(2)}, u32[]{:S(2)}) collective-permute-start(bf16[4,128,256]{2,1,0:T(8,128)(2,1)S(1)} %collective-permute-done.5.refs_1_), channel_id=1, source_target_pairs={{0,112},{4,116},{8,120},{12,124},{16,32},{20,36},{24,40},{28,44},{... | collective-permute-start | bytes 786440 | tf_op jit(solution)/shard_map/ppermute | solution.py:28
  55.3 2.0 %attend.6 = (f32[1024,256]{1,0:T(8,128)S(1)}, f32[1024,128]{1,0:T(8,128)S(1)}) custom-call(bf16[1024,256]{1,0:T(8,128)(2,1)S(1)} %get-tuple-element.19.q_all, bf16[4096,128]{1,0:T(8,128)(2,1)S(1)} %get-tuple-element.20.bias_ref, bf16[4,128,256]{2,1,0:T(8,128)(2,1)S(1)} %collective-permute-done.1.refs_0_, ...), custom_call_target="tpu_custom_call" | custom-call | flops 4294967296 | bytes 4194304 | tf_op jit(solution)/shard_map/attend/pallas_call | solution.py:178
  57.3 1.9 %collective-permute-start.3 = (bf16[2,128,256]{2,1,0:T(8,128)(2,1)S(1)}, bf16[2,128,256]{2,1,0:T(8,128)(2,1)S(1)}, u32[]{:S(2)}, u32[]{:S(2)}) collective-permute-start(bf16[2,128,256]{2,1,0:T(8,128)(2,1)S(1)} %slice.8), channel_id=1, source_target_pairs={{0,112},{4,116},{8,120},{12,124},{16,32},{20,36},{24,40},{28,44},{... | collective-permute-start | bytes 393224 | tf_op jit(solution)/shard_map/ppermute | solution.py:28
  59.2 1.0 %collective-permute-done.6.refs_1_ = bf16[4,128,256]{2,1,0:T(8,128)(2,1)S(1)} collective-permute-done((bf16[4,128,256]{2,1,0:T(8,128)(2,1)S(1)}, bf16[4,128,256]{2,1,0:T(8,128)(2,1)S(1)}, u32[]{:S(2)}, u32[]{:S(2)}) %collective-permute-start.6) | collective-permute-done | bytes 262176 | tf_op jit(solution)/shard_map/ppermute | solution.py:28
  60.2 1.9 %collective-permute-start.7 = (bf16[2,128,256]{2,1,0:T(8,128)(2,1)S(1)}, bf16[2,128,256]{2,1,0:T(8,128)(2,1)S(1)}, u32[]{:S(2)}, u32[]{:S(2)}) collective-permute-start(bf16[2,128,256]{2,1,0:T(8,128)(2,1)S(1)} %slice.9), channel_id=1, source_target_pairs={{0,16},{4,20},{8,24},{12,28},{16,0},{20,4},{24,8},{28,12},{32,48},... | collective-permute-start | bytes 393224 | tf_op jit(solution)/shard_map/ppermute | solution.py:28
  62.2 2.0 %attend.7 = (f32[1024,256]{1,0:T(8,128)S(1)}, f32[1024,128]{1,0:T(8,128)S(1)}) custom-call(bf16[1024,256]{1,0:T(8,128)(2,1)S(1)} %get-tuple-element.19.q_all, bf16[4096,128]{1,0:T(8,128)(2,1)S(1)} %get-tuple-element.20.bias_ref, bf16[4,128,256]{2,1,0:T(8,128)(2,1)S(1)} %collective-permute-done.2.refs_0_, ...), custom_call_target="tpu_custom_call" | custom-call | flops 4294967296 | bytes 4194304 | tf_op jit(solution)/shard_map/attend/pallas_call | solution.py:178
  64.2 1.2 %collective-permute-done.3.refs_0_ = bf16[2,128,256]{2,1,0:T(8,128)(2,1)S(1)} collective-permute-done((bf16[2,128,256]{2,1,0:T(8,128)(2,1)S(1)}, bf16[2,128,256]{2,1,0:T(8,128)(2,1)S(1)}, u32[]{:S(2)}, u32[]{:S(2)}) %collective-permute-start.3) | collective-permute-done | bytes 131104 | tf_op jit(solution)/shard_map/ppermute | solution.py:28
  65.4 1.7 %collective-permute-done.7.refs_1_ = bf16[2,128,256]{2,1,0:T(8,128)(2,1)S(1)} collective-permute-done((bf16[2,128,256]{2,1,0:T(8,128)(2,1)S(1)}, bf16[2,128,256]{2,1,0:T(8,128)(2,1)S(1)}, u32[]{:S(2)}, u32[]{:S(2)}) %collective-permute-start.7) | collective-permute-done | bytes 131104 | tf_op jit(solution)/shard_map/ppermute | solution.py:28
  67.1 2.2 %attend_last.1 = (bf16[128,1024]{1,0:T(8,128)(2,1)}, bf16[4,32,1536]{2,1,0:T(8,128)(2,1)S(1)}) custom-call(bf16[1024,256]{1,0:T(8,128)(2,1)S(1)} %get-tuple-element.19.q_all, bf16[4096,128]{1,0:T(8,128)(2,1)S(1)} %get-tuple-element.20.bias_ref, bf16[2,128,256]{2,1,0:T(8,128)(2,1)S(1)} %collective-permute-done.3.refs_0_, ...), custom_call_target="tpu_custom_call" | custom-call | flops 2147483648 | bytes 4194304 | tf_op jit(solution)/shard_map/attend_last/pallas_call | solution.py:178
  69.3 10.7 %all_to_all.10.part_ref = bf16[4,32,1536]{2,1,0:T(8,128)(2,1)} all-to-all(bf16[4,32,1536]{2,1,0:T(8,128)(2,1)S(1)} %get-tuple-element.31), channel_id=1, replica_groups=mesh['dp'=4,'ctx'=32,'tp'=4] {'tp'}, dimensions={0} | all-to-all | bytes 786432 | tf_op jit(solution)/shard_map/all_to_all | solution.py:236
  79.9 1.8 %ratio.1 = f32[1,128]{1,0:T(1,128)} custom-call(s32[2]{0:T(128)} %copy-done, bf16[4,32,1536]{2,1,0:T(8,128)(2,1)} %all_to_all.10.part_ref, s32[1,128]{1,0:T(1,128)} %bitcast.5, f32[1,128]{1,0:T(1,128)} %bitcast.6), custom_call_target="tpu_custom_call" | custom-call | tf_op jit(solution)/shard_map/ratio/pallas_call | solution.py:238
  81.8 9.8 %psum.7 = f32[128]{0:T(128)} all-reduce(f32[128]{0:T(128)} %bitcast.7), channel_id=1, replica_groups=mesh['dp'=4,'ctx'=32,'tp'=4] {'tp'}, use_global_device_ids=true, to_apply=%region_0.0 | all-reduce | flops 128 | bytes 1024 | tf_op jit(solution)/shard_map/psum | solution.py:245
  (15 shorter events, 2.5 us)
Async XLA Ops:
  2.1 17.5 %all-to-all-start = ((bf16[4,128,256]{2,1,0:T(8,128)(2,1)}), bf16[4,128,256]{2,1,0:T(8,128)(2,1)S(1)}, u32[]{:S(2)}, u32[]{:S(2)}) async-start(bf16[4,128,256]{2,1,0:T(8,128)(2,1)} %pack.1), calls=%async_computation | async-start | bytes 524288 | tf_op jit(solution)/shard_map/all_to_all | solution.py:217
  9.3 0.9 %copy-start.2 = (bf16[128,1024]{1,0:T(8,128)(2,1)S(1)}, bf16[128,1024]{1,0:T(8,128)(2,1)}, u32[]{:S(2)}) copy-start(bf16[128,1024]{1,0:T(8,128)(2,1)} %q_ref.1) | copy-start | bytes 786436
  10.3 0.7 copy-start.3
  10.9 0.9 %copy-start = (s32[2]{0:T(128)}, s32[2]{0:T(128)S(1)}, u32[]{:S(2)}) copy-start(s32[2]{0:T(128)S(1)} %pad_add_fusion.ids) | copy-start | bytes 28
  19.7 14.4 %collective-permute-start = (bf16[4,128,256]{2,1,0:T(8,128)(2,1)S(1)}, bf16[4,128,256]{2,1,0:T(8,128)(2,1)S(1)}, u32[]{:S(2)}, u32[]{:S(2)}) collective-permute-start(bf16[4,128,256]{2,1,0:T(8,128)(2,1)S(1)} %all-to-all-done.refs_0_), channel_id=1, source_target_pairs={{0,16},{4,20},{8,24},{12,28},{16,0},{20,4},{24,8},{28,12},{32,48},... | collective-permute-start | bytes 786440 | tf_op jit(solution)/shard_map/ppermute | solution.py:28
  24.0 14.9 %collective-permute-start.4 = (bf16[4,128,256]{2,1,0:T(8,128)(2,1)S(1)}, bf16[4,128,256]{2,1,0:T(8,128)(2,1)S(1)}, u32[]{:S(2)}, u32[]{:S(2)}) collective-permute-start(bf16[4,128,256]{2,1,0:T(8,128)(2,1)S(1)} %all-to-all-done.refs_0_), channel_id=1, source_target_pairs={{0,112},{4,116},{8,120},{12,124},{16,32},{20,36},{24,40},{28,44},{... | collective-permute-start | bytes 786440 | tf_op jit(solution)/shard_map/ppermute | solution.py:28
  34.1 9.5 %collective-permute-start.1 = (bf16[4,128,256]{2,1,0:T(8,128)(2,1)S(1)}, bf16[4,128,256]{2,1,0:T(8,128)(2,1)S(1)}, u32[]{:S(2)}, u32[]{:S(2)}) collective-permute-start(bf16[4,128,256]{2,1,0:T(8,128)(2,1)S(1)} %collective-permute-done.refs_0_), channel_id=1, source_target_pairs={{0,112},{4,116},{8,120},{12,124},{16,32},{20,36},{24,40},{28,44},{... | collective-permute-start | bytes 786440 | tf_op jit(solution)/shard_map/ppermute | solution.py:28
  38.9 10.9 %collective-permute-start.5 = (bf16[4,128,256]{2,1,0:T(8,128)(2,1)S(1)}, bf16[4,128,256]{2,1,0:T(8,128)(2,1)S(1)}, u32[]{:S(2)}, u32[]{:S(2)}) collective-permute-start(bf16[4,128,256]{2,1,0:T(8,128)(2,1)S(1)} %collective-permute-done.4.refs_1_), channel_id=1, source_target_pairs={{0,16},{4,20},{8,24},{12,28},{16,0},{20,4},{24,8},{28,12},{32,48},... | collective-permute-start | bytes 786440 | tf_op jit(solution)/shard_map/ppermute | solution.py:28
  43.6 13.7 %collective-permute-start.2 = (bf16[4,128,256]{2,1,0:T(8,128)(2,1)S(1)}, bf16[4,128,256]{2,1,0:T(8,128)(2,1)S(1)}, u32[]{:S(2)}, u32[]{:S(2)}) collective-permute-start(bf16[4,128,256]{2,1,0:T(8,128)(2,1)S(1)} %collective-permute-done.1.refs_0_), channel_id=1, source_target_pairs={{0,16},{4,20},{8,24},{12,28},{16,0},{20,4},{24,8},{28,12},{32,48},... | collective-permute-start | bytes 786440 | tf_op jit(solution)/shard_map/ppermute | solution.py:28
  49.8 10.5 %collective-permute-start.6 = (bf16[4,128,256]{2,1,0:T(8,128)(2,1)S(1)}, bf16[4,128,256]{2,1,0:T(8,128)(2,1)S(1)}, u32[]{:S(2)}, u32[]{:S(2)}) collective-permute-start(bf16[4,128,256]{2,1,0:T(8,128)(2,1)S(1)} %collective-permute-done.5.refs_1_), channel_id=1, source_target_pairs={{0,112},{4,116},{8,120},{12,124},{16,32},{20,36},{24,40},{28,44},{... | collective-permute-start | bytes 786440 | tf_op jit(solution)/shard_map/ppermute | solution.py:28
  57.3 8.1 %collective-permute-start.3 = (bf16[2,128,256]{2,1,0:T(8,128)(2,1)S(1)}, bf16[2,128,256]{2,1,0:T(8,128)(2,1)S(1)}, u32[]{:S(2)}, u32[]{:S(2)}) collective-permute-start(bf16[2,128,256]{2,1,0:T(8,128)(2,1)S(1)} %slice.8), channel_id=1, source_target_pairs={{0,112},{4,116},{8,120},{12,124},{16,32},{20,36},{24,40},{28,44},{... | collective-permute-start | bytes 393224 | tf_op jit(solution)/shard_map/ppermute | solution.py:28
  60.2 6.9 %collective-permute-start.7 = (bf16[2,128,256]{2,1,0:T(8,128)(2,1)S(1)}, bf16[2,128,256]{2,1,0:T(8,128)(2,1)S(1)}, u32[]{:S(2)}, u32[]{:S(2)}) collective-permute-start(bf16[2,128,256]{2,1,0:T(8,128)(2,1)S(1)} %slice.9), channel_id=1, source_target_pairs={{0,16},{4,20},{8,24},{12,28},{16,0},{20,4},{24,8},{28,12},{32,48},... | collective-permute-start | bytes 393224 | tf_op jit(solution)/shard_map/ppermute | solution.py:28
  62.2 4.9 %copy-start.1 = (bf16[1024,1536]{1,0:T(8,128)(2,1)S(1)}, bf16[1024,1536]{1,0:T(8,128)(2,1)}, u32[]{:S(2)}) copy-start(bf16[1024,1536]{1,0:T(8,128)(2,1)} %refs_4_.1) | copy-start | bytes 9437188

commit v3 on v2

--- a/solution.py
+++ b/solution.py
@@ -132,9 +132,18 @@
     v = jnp.concatenate([r[:, :, HEAD:].reshape(-1, HEAD) for r in kv_refs], axis=0)
     k_ext = jnp.concatenate([k, bias_ref[start : start + k.shape[0], :]], axis=1)
     v_ext = jnp.concatenate([v, jnp.ones_like(v)], axis=1)
-    for r in range(total // ROW_TILE):
+    tiles = total // ROW_TILE
+
+    def scores(r):
         at = slice(r * ROW_TILE, (r + 1) * ROW_TILE)
-        s = lax.dot_general(q_all[at, :], k_ext, (((1,), (1,)), ((), ())), preferred_element_type=jnp.float32)
+        return lax.dot_general(q_all[at, :], k_ext, (((1,), (1,)), ((), ())), preferred_element_type=jnp.float32)
+
+    ahead = scores(0)
+    for r in range(tiles):
+        at = slice(r * ROW_TILE, (r + 1) * ROW_TILE)
+        s = ahead
+        if r + 1 < tiles:
+            ahead = scores(r + 1)
         peak = jnp.max(s, axis=1, keepdims=True)
         if not first:
             old = peak_in[at, :1]
@@ -206,43 +215,43 @@
     peak = jnp.max(x, axis=1, keepdims=True)
     mass = jnp.sum(jnp.exp(x - peak), axis=1, keepdims=True)
     ratio = target - (peak + jnp.log(mass))
-    out_ref[...] = jnp.sum(jnp.where(mine, ratio - logp_ref[...], 0.0), axis=0, keepdims=True)
+    mine_row = jnp.sum(jnp.where(mine, ratio - logp_ref[...], 0.0), axis=0, keepdims=True)
+    out_ref[...] = jnp.broadcast_to(mine_row[None], out_ref.shape)
 
 
 def body(queries, keys, values, readout, token_ids, stored_logp, span_order):
     rows = queries.shape[0]
-    ids = jnp.stack([lax.axis_index("ctx"), lax.axis_index("tp")]).astype(jnp.int32)
+    ids = jnp.stack([lax.axis_index(axis) for axis in ("ctx", "tp")]).astype(jnp.int32)
     q_all, bias = prep(ids, span_order, queries)
 
     kv = lax.all_to_all(pack(keys, values), "ctx", 0, 0, axis_index_groups=Y_GROUPS, tiled=True)
     kv, q_all, bias = lax.optimization_barrier((kv, q_all, bias))
     a, b = swap_z(kv, 0), swap_z(kv, 1)
-    start = Y * rows
+    per = Y * rows
     state = attend(q_all, bias, [kv], 0)
-    now = [a, b]
-    a, b = swap_z(a, 1), swap_z(b, 0)
-    for step in range(2, Z // 2 + 1):
-        last = step == Z // 2
-        state = attend(q_all, bias, now, start, state)
-        start += 2 * Y * rows
-        if last:
-            break
-        now = [a, b]
-        if step == Z // 2 - 1:
-            a, b = a[: Y // 2], b[Y // 2 :]
-        a, b = swap_z(a, step % 2), swap_z(b, 1 - step % 2)
-    attended, parts = attend(q_all, bias, [a, b], start, state, readout)
+    a2, b2 = swap_z(a, 1), swap_z(b, 0)
+    _, state = lax.optimization_barrier((a2, state))
+    state = attend(q_all, bias, [a, b], per, state)
+    a3 = swap_z(a2, 0)
+    held, state = lax.optimization_barrier((b2, state))
+    b3 = swap_z(held, 1)
+    _, state = lax.optimization_barrier((a3, state))
+    state = attend(q_all, bias, [a2, b2], 3 * per, state)
+    a4 = swap_z(a3, 1)
+    state = attend(q_all, bias, [a3, b3], 5 * per, state)
+    attended, parts = attend(q_all, bias, [a4], 7 * per, state, readout)
 
     parts = lax.all_to_all(parts, "tp", 0, 0, tiled=True)
     args = [parts, token_ids.reshape(1, rows), stored_logp.reshape(1, rows)]
     ratio = pl.pallas_call(
         ratio_kernel,
-        out_shape=jax.ShapeDtypeStruct((1, rows), jnp.float32),
+        out_shape=jax.ShapeDtypeStruct((TP, 1, rows), jnp.float32),
         in_specs=[SMEM] + [VMEM] * len(args),
         out_specs=VMEM,
         name="ratio",
     )(ids, *args)
-    return attended, lax.psum(ratio.reshape(rows), "tp")
+    ratio = lax.all_to_all(ratio, "tp", 0, 0, tiled=True)
+    return attended, jnp.sum(ratio, axis=(0, 1))
 
 
 def solution(mesh):

time: 92.1 us -> 91 us (0.988)
  the two profiles are of different devices: /device:TPU:2 before, /device:TPU:16 now
where the time goes in v3:
time: 91 us; the launch traced here: 90.4 us
  starting transfers between devices  39.4 us (43%)
  blocking collectives  19.9 us (22%)
  waiting for transfers between devices  15.7 us (17%)
  Pallas kernels  12.4 us (14%)
  local copies, waits for them, and re-layouts  1.61 us (2%)
    ppermute x7, starting transfers between devices, swap_z(): return lax.ppermute(x, 'ctx', pairs)  30.3 us
    all_to_all x1, blocking collectives, body(): parts = lax.all_to_all(parts, 'tp', 0, 0, tiled=True)  11.6 us
    ppermute x7, waiting for transfers between devices, swap_z(): return lax.ppermute(x, 'ctx', pairs)  10.5 us
    all_to_all x1, starting transfers between devices, body(): lax.all_to_all(pack(keys, values), 'ctx', 0, 0, axis_index_groups=Y_GROUP...  9.1 us
    all_to_all x1, blocking collectives, body(): ratio = lax.all_to_all(ratio, 'tp', 0, 0, tiled=True)  8.29 us
    pallas_call x5, Pallas kernels, attend(): pl.pallas_call(functools.partial(attend_kernel, start, len(kvs), first, l...  8.13 us
    all_to_all x1, waiting for transfers between devices, body(): lax.all_to_all(pack(keys, values), 'ctx', 0, 0, axis_index_groups=Y_GROUP...  5.25 us
    pallas_call x1, Pallas kernels, body(): pl.pallas_call(ratio_kernel, out_shape=jax.ShapeDtypeStruct((TP, 1, rows)...  1.85 us
  transfers between devices with their start and end apart: 8, of which 6 were waited for; matrix products, arithmetic and copies ran while one was open for 0% of the time, Pallas kernels for 8%

profile of v3, /device:TPU:16, one launch (start us, length us, event | category | flops | bytes accessed | tf_op | source)
XLA Modules:
  0.0 90.4 jit_solution(12778596904485924889)
XLA Ops:
  0.6 1.5 %pack.1 = bf16[4,128,256]{2,1,0:T(8,128)(2,1)} custom-call(bf16[128,128]{1,0:T(8,128)(2,1)} %k_ref.1, bf16[128,128]{1,0:T(8,128)(2,1)} %v_ref.1), custom_call_target="tpu_custom_call" | custom-call | tf_op jit(solution)/shard_map/pack/pallas_call | solution.py:62
  2.1 9.1 %all-to-all-start = ((bf16[4,128,256]{2,1,0:T(8,128)(2,1)}), bf16[4,128,256]{2,1,0:T(8,128)(2,1)S(1)}, u32[]{:S(2)}, u32[]{:S(2)}) async-start(bf16[4,128,256]{2,1,0:T(8,128)(2,1)} %pack.1), calls=%async_computation | async-start | bytes 524288 | tf_op jit(solution)/shard_map/all_to_all | solution.py:227
  11.3 0.9 %copy-done.2 = bf16[128,1024]{1,0:T(8,128)(2,1)S(1)} copy-done((bf16[128,1024]{1,0:T(8,128)(2,1)S(1)}, bf16[128,1024]{1,0:T(8,128)(2,1)}, u32[]{:S(2)}) %copy-start.2) | copy-done | bytes 262168
  13.9 5.2 %all-to-all-done.refs_0_ = bf16[4,128,256]{2,1,0:T(8,128)(2,1)S(1)} async-done(((bf16[4,128,256]{2,1,0:T(8,128)(2,1)}), bf16[4,128,256]{2,1,0:T(8,128)(2,1)S(1)}, u32[]{:S(2)}, u32[]{:S(2)}) %all-to-all-start) | async-done | bytes 262176 | tf_op jit(solution)/shard_map/all_to_all | solution.py:227
  19.1 4.3 %collective-permute-start = (bf16[4,128,256]{2,1,0:T(8,128)(2,1)S(1)}, bf16[4,128,256]{2,1,0:T(8,128)(2,1)S(1)}, u32[]{:S(2)}, u32[]{:S(2)}) collective-permute-start(bf16[4,128,256]{2,1,0:T(8,128)(2,1)S(1)} %all-to-all-done.refs_0_), channel_id=1, source_target_pairs={{0,16},{4,20},{8,24},{12,28},{16,0},{20,4},{24,8},{28,12},{32,48},... | collective-permute-start | bytes 786440 | tf_op jit(solution)/shard_map/ppermute | solution.py:28
  23.4 9.1 %collective-permute-start.4 = (bf16[4,128,256]{2,1,0:T(8,128)(2,1)S(1)}, bf16[4,128,256]{2,1,0:T(8,128)(2,1)S(1)}, u32[]{:S(2)}, u32[]{:S(2)}) collective-permute-start(bf16[4,128,256]{2,1,0:T(8,128)(2,1)S(1)} %all-to-all-done.refs_0_), channel_id=1, source_target_pairs={{0,112},{4,116},{8,120},{12,124},{16,32},{20,36},{24,40},{28,44},{... | collective-permute-start | bytes 786440 | tf_op jit(solution)/shard_map/ppermute | solution.py:28
  32.5 7.4 %collective-permute-start.1 = (bf16[4,128,256]{2,1,0:T(8,128)(2,1)S(1)}, bf16[4,128,256]{2,1,0:T(8,128)(2,1)S(1)}, u32[]{:S(2)}, u32[]{:S(2)}) collective-permute-start(bf16[4,128,256]{2,1,0:T(8,128)(2,1)S(1)} %collective-permute-done.refs_0_), channel_id=1, source_target_pairs={{0,112},{4,116},{8,120},{12,124},{16,32},{20,36},{24,40},{28,44},{... | collective-permute-start | bytes 786440 | tf_op jit(solution)/shard_map/ppermute | solution.py:28
  39.9 1.0 %attend.4 = (f32[1024,256]{1,0:T(8,128)S(1)}, f32[1024,128]{1,0:T(8,128)S(1)}) custom-call(bf16[1024,256]{1,0:T(8,128)(2,1)S(1)} %get-tuple-element.26.q_all, bf16[4096,128]{1,0:T(8,128)(2,1)S(1)} %get-tuple-element.27.bias_ref, bf16[4,128,256]{2,1,0:T(8,128)(2,1)S(1)} %all-to-all-done.refs_0_), custom_call_target="tpu_custom_call" | custom-call | flops 2147483648 | bytes 4194304 | tf_op jit(solution)/shard_map/attend/pallas_call | solution.py:187
  40.9 1.9 %collective-permute-start.5 = (bf16[4,128,256]{2,1,0:T(8,128)(2,1)S(1)}, bf16[4,128,256]{2,1,0:T(8,128)(2,1)S(1)}, u32[]{:S(2)}, u32[]{:S(2)}) collective-permute-start(bf16[4,128,256]{2,1,0:T(8,128)(2,1)S(1)} %collective-permute-done.4.refs_1_), channel_id=1, source_target_pairs={{0,16},{4,20},{8,24},{12,28},{16,0},{20,4},{24,8},{28,12},{32,48},... | collective-permute-start | bytes 786440 | tf_op jit(solution)/shard_map/ppermute | solution.py:28
  42.8 2.4 %collective-permute-done.1.refs_0_ = bf16[4,128,256]{2,1,0:T(8,128)(2,1)S(1)} collective-permute-done((bf16[4,128,256]{2,1,0:T(8,128)(2,1)S(1)}, bf16[4,128,256]{2,1,0:T(8,128)(2,1)S(1)}, u32[]{:S(2)}, u32[]{:S(2)}) %collective-permute-start.1) | collective-permute-done | bytes 262176 | tf_op jit(solution)/shard_map/ppermute | solution.py:28
  45.3 1.9 %collective-permute-start.2 = (bf16[4,128,256]{2,1,0:T(8,128)(2,1)S(1)}, bf16[4,128,256]{2,1,0:T(8,128)(2,1)S(1)}, u32[]{:S(2)}, u32[]{:S(2)}) collective-permute-start(bf16[4,128,256]{2,1,0:T(8,128)(2,1)S(1)} %collective-permute-done.1.refs_0_), channel_id=1, source_target_pairs={{0,16},{4,20},{8,24},{12,28},{16,0},{20,4},{24,8},{28,12},{32,48},... | collective-permute-start | bytes 786440 | tf_op jit(solution)/shard_map/ppermute | solution.py:28
  47.2 1.8 %attend.5 = (f32[1024,256]{1,0:T(8,128)S(1)}, f32[1024,128]{1,0:T(8,128)S(1)}) custom-call(bf16[1024,256]{1,0:T(8,128)(2,1)S(1)} %get-tuple-element.26.q_all, bf16[4096,128]{1,0:T(8,128)(2,1)S(1)} %get-tuple-element.27.bias_ref, bf16[4,128,256]{2,1,0:T(8,128)(2,1)S(1)} %collective-permute-done.refs_0_, ...), custom_call_target="tpu_custom_call" | custom-call | flops 4294967296 | bytes 4194304 | tf_op jit(solution)/shard_map/attend/pallas_call | solution.py:187
  48.9 2.2 %collective-permute-done.5.refs_1_ = bf16[4,128,256]{2,1,0:T(8,128)(2,1)S(1)} collective-permute-done((bf16[4,128,256]{2,1,0:T(8,128)(2,1)S(1)}, bf16[4,128,256]{2,1,0:T(8,128)(2,1)S(1)}, u32[]{:S(2)}, u32[]{:S(2)}) %collective-permute-start.5) | collective-permute-done | bytes 262176 | tf_op jit(solution)/shard_map/ppermute | solution.py:28
  51.2 2.6 %collective-permute-start.6 = (bf16[4,128,256]{2,1,0:T(8,128)(2,1)S(1)}, bf16[4,128,256]{2,1,0:T(8,128)(2,1)S(1)}, u32[]{:S(2)}, u32[]{:S(2)}) collective-permute-start(bf16[4,128,256]{2,1,0:T(8,128)(2,1)S(1)} %collective-permute-done.5.refs_1_), channel_id=1, source_target_pairs={{0,112},{4,116},{8,120},{12,124},{16,32},{20,36},{24,40},{28,44},{... | collective-permute-start | bytes 786440 | tf_op jit(solution)/shard_map/ppermute | solution.py:28
  53.8 1.4 %collective-permute-done.2.refs_0_ = bf16[4,128,256]{2,1,0:T(8,128)(2,1)S(1)} collective-permute-done((bf16[4,128,256]{2,1,0:T(8,128)(2,1)S(1)}, bf16[4,128,256]{2,1,0:T(8,128)(2,1)S(1)}, u32[]{:S(2)}, u32[]{:S(2)}) %collective-permute-start.2) | collective-permute-done | bytes 262176 | tf_op jit(solution)/shard_map/ppermute | solution.py:28
  55.2 3.1 %collective-permute-start.3 = (bf16[4,128,256]{2,1,0:T(8,128)(2,1)S(1)}, bf16[4,128,256]{2,1,0:T(8,128)(2,1)S(1)}, u32[]{:S(2)}, u32[]{:S(2)}) collective-permute-start(bf16[4,128,256]{2,1,0:T(8,128)(2,1)S(1)} %collective-permute-done.2.refs_0_), channel_id=1, source_target_pairs={{0,112},{4,116},{8,120},{12,124},{16,32},{20,36},{24,40},{28,44},{... | collective-permute-start | bytes 786440 | tf_op jit(solution)/shard_map/ppermute | solution.py:28
  58.4 1.8 %attend.6 = (f32[1024,256]{1,0:T(8,128)S(1)}, f32[1024,128]{1,0:T(8,128)S(1)}) custom-call(bf16[1024,256]{1,0:T(8,128)(2,1)S(1)} %get-tuple-element.26.q_all, bf16[4096,128]{1,0:T(8,128)(2,1)S(1)} %get-tuple-element.27.bias_ref, bf16[4,128,256]{2,1,0:T(8,128)(2,1)S(1)} %collective-permute-done.1.refs_0_, ...), custom_call_target="tpu_custom_call" | custom-call | flops 4294967296 | bytes 4194304 | tf_op jit(solution)/shard_map/attend/pallas_call | solution.py:187
  60.1 1.6 %collective-permute-done.6.refs_1_ = bf16[4,128,256]{2,1,0:T(8,128)(2,1)S(1)} collective-permute-done((bf16[4,128,256]{2,1,0:T(8,128)(2,1)S(1)}, bf16[4,128,256]{2,1,0:T(8,128)(2,1)S(1)}, u32[]{:S(2)}, u32[]{:S(2)}) %collective-permute-start.6) | collective-permute-done | bytes 262176 | tf_op jit(solution)/shard_map/ppermute | solution.py:28
  61.8 1.7 %attend.7 = (f32[1024,256]{1,0:T(8,128)S(1)}, f32[1024,128]{1,0:T(8,128)S(1)}) custom-call(bf16[1024,256]{1,0:T(8,128)(2,1)S(1)} %get-tuple-element.26.q_all, bf16[4096,128]{1,0:T(8,128)(2,1)S(1)} %get-tuple-element.27.bias_ref, bf16[4,128,256]{2,1,0:T(8,128)(2,1)S(1)} %collective-permute-done.2.refs_0_, ...), custom_call_target="tpu_custom_call" | custom-call | flops 4294967296 | bytes 4194304 | tf_op jit(solution)/shard_map/attend/pallas_call | solution.py:187
  63.5 2.7 %collective-permute-done.3.refs_0_ = bf16[4,128,256]{2,1,0:T(8,128)(2,1)S(1)} collective-permute-done((bf16[4,128,256]{2,1,0:T(8,128)(2,1)S(1)}, bf16[4,128,256]{2,1,0:T(8,128)(2,1)S(1)}, u32[]{:S(2)}, u32[]{:S(2)}) %collective-permute-start.3) | collective-permute-done | bytes 262176 | tf_op jit(solution)/shard_map/ppermute | solution.py:28
  66.3 1.9 %attend_last.1 = (bf16[128,1024]{1,0:T(8,128)(2,1)}, bf16[4,32,1536]{2,1,0:T(8,128)(2,1)S(1)}) custom-call(bf16[1024,256]{1,0:T(8,128)(2,1)S(1)} %get-tuple-element.26.q_all, bf16[4096,128]{1,0:T(8,128)(2,1)S(1)} %get-tuple-element.27.bias_ref, bf16[4,128,256]{2,1,0:T(8,128)(2,1)S(1)} %collective-permute-done.3.refs_0_, ...), custom_call_target="tpu_custom_call" | custom-call | flops 2147483648 | bytes 4194304 | tf_op jit(solution)/shard_map/attend_last/pallas_call | solution.py:187
  68.2 11.6 %all_to_all.15.part_ref = bf16[4,32,1536]{2,1,0:T(8,128)(2,1)} all-to-all(bf16[4,32,1536]{2,1,0:T(8,128)(2,1)S(1)} %get-tuple-element.45), channel_id=1, replica_groups=mesh['dp'=4,'ctx'=32,'tp'=4] {'tp'}, dimensions={0} | all-to-all | bytes 786432 | tf_op jit(solution)/shard_map/all_to_all | solution.py:244
  79.7 1.9 %ratio.1 = f32[4,1,128]{2,1,0:T(1,128)} custom-call(s32[2]{0:T(128)} %copy-done, bf16[4,32,1536]{2,1,0:T(8,128)(2,1)} %all_to_all.15.part_ref, s32[1,128]{1,0:T(1,128)} %bitcast.4, f32[1,128]{1,0:T(1,128)} %bitcast.5), custom_call_target="tpu_custom_call" | custom-call | tf_op jit(solution)/shard_map/ratio/pallas_call | solution.py:246
  81.6 8.3 %all_to_all.16 = f32[4,1,128]{2,1,0:T(1,128)S(1)} all-to-all(f32[4,1,128]{2,1,0:T(1,128)} %ratio.1), channel_id=1, replica_groups=mesh['dp'=4,'ctx'=32,'tp'=4] {'tp'}, dimensions={0} | all-to-all | bytes 4096 | tf_op jit(solution)/shard_map/all_to_all | solution.py:253
  (12 shorter events, 2.2 us)
Async XLA Ops:
  2.1 17.0 %all-to-all-start = ((bf16[4,128,256]{2,1,0:T(8,128)(2,1)}), bf16[4,128,256]{2,1,0:T(8,128)(2,1)S(1)}, u32[]{:S(2)}, u32[]{:S(2)}) async-start(bf16[4,128,256]{2,1,0:T(8,128)(2,1)} %pack.1), calls=%async_computation | async-start | bytes 524288 | tf_op jit(solution)/shard_map/all_to_all | solution.py:227
  11.3 0.9 %copy-start.2 = (bf16[128,1024]{1,0:T(8,128)(2,1)S(1)}, bf16[128,1024]{1,0:T(8,128)(2,1)}, u32[]{:S(2)}) copy-start(bf16[128,1024]{1,0:T(8,128)(2,1)} %q_ref.1) | copy-start | bytes 786436
  12.3 0.7 copy-start.3
  12.9 0.9 %copy-start = (s32[2]{0:T(128)}, s32[2]{0:T(128)S(1)}, u32[]{:S(2)}) copy-start(s32[2]{0:T(128)S(1)} %pad_add_fusion.ids) | copy-start | bytes 28
  19.1 13.4 %collective-permute-start = (bf16[4,128,256]{2,1,0:T(8,128)(2,1)S(1)}, bf16[4,128,256]{2,1,0:T(8,128)(2,1)S(1)}, u32[]{:S(2)}, u32[]{:S(2)}) collective-permute-start(bf16[4,128,256]{2,1,0:T(8,128)(2,1)S(1)} %all-to-all-done.refs_0_), channel_id=1, source_target_pairs={{0,16},{4,20},{8,24},{12,28},{16,0},{20,4},{24,8},{28,12},{32,48},... | collective-permute-start | bytes 786440 | tf_op jit(solution)/shard_map/ppermute | solution.py:28
  23.4 17.5 %collective-permute-start.4 = (bf16[4,128,256]{2,1,0:T(8,128)(2,1)S(1)}, bf16[4,128,256]{2,1,0:T(8,128)(2,1)S(1)}, u32[]{:S(2)}, u32[]{:S(2)}) collective-permute-start(bf16[4,128,256]{2,1,0:T(8,128)(2,1)S(1)} %all-to-all-done.refs_0_), channel_id=1, source_target_pairs={{0,112},{4,116},{8,120},{12,124},{16,32},{20,36},{24,40},{28,44},{... | collective-permute-start | bytes 786440 | tf_op jit(solution)/shard_map/ppermute | solution.py:28
  32.5 12.7 %collective-permute-start.1 = (bf16[4,128,256]{2,1,0:T(8,128)(2,1)S(1)}, bf16[4,128,256]{2,1,0:T(8,128)(2,1)S(1)}, u32[]{:S(2)}, u32[]{:S(2)}) collective-permute-start(bf16[4,128,256]{2,1,0:T(8,128)(2,1)S(1)} %collective-permute-done.refs_0_), channel_id=1, source_target_pairs={{0,112},{4,116},{8,120},{12,124},{16,32},{20,36},{24,40},{28,44},{... | collective-permute-start | bytes 786440 | tf_op jit(solution)/shard_map/ppermute | solution.py:28
  40.9 10.3 %collective-permute-start.5 = (bf16[4,128,256]{2,1,0:T(8,128)(2,1)S(1)}, bf16[4,128,256]{2,1,0:T(8,128)(2,1)S(1)}, u32[]{:S(2)}, u32[]{:S(2)}) collective-permute-start(bf16[4,128,256]{2,1,0:T(8,128)(2,1)S(1)} %collective-permute-done.4.refs_1_), channel_id=1, source_target_pairs={{0,16},{4,20},{8,24},{12,28},{16,0},{20,4},{24,8},{28,12},{32,48},... | collective-permute-start | bytes 786440 | tf_op jit(solution)/shard_map/ppermute | solution.py:28
  45.3 10.0 %collective-permute-start.2 = (bf16[4,128,256]{2,1,0:T(8,128)(2,1)S(1)}, bf16[4,128,256]{2,1,0:T(8,128)(2,1)S(1)}, u32[]{:S(2)}, u32[]{:S(2)}) collective-permute-start(bf16[4,128,256]{2,1,0:T(8,128)(2,1)S(1)} %collective-permute-done.1.refs_0_), channel_id=1, source_target_pairs={{0,16},{4,20},{8,24},{12,28},{16,0},{20,4},{24,8},{28,12},{32,48},... | collective-permute-start | bytes 786440 | tf_op jit(solution)/shard_map/ppermute | solution.py:28
  51.2 10.6 %collective-permute-start.6 = (bf16[4,128,256]{2,1,0:T(8,128)(2,1)S(1)}, bf16[4,128,256]{2,1,0:T(8,128)(2,1)S(1)}, u32[]{:S(2)}, u32[]{:S(2)}) collective-permute-start(bf16[4,128,256]{2,1,0:T(8,128)(2,1)S(1)} %collective-permute-done.5.refs_1_), channel_id=1, source_target_pairs={{0,112},{4,116},{8,120},{12,124},{16,32},{20,36},{24,40},{28,44},{... | collective-permute-start | bytes 786440 | tf_op jit(solution)/shard_map/ppermute | solution.py:28
  55.2 11.0 %collective-permute-start.3 = (bf16[4,128,256]{2,1,0:T(8,128)(2,1)S(1)}, bf16[4,128,256]{2,1,0:T(8,128)(2,1)S(1)}, u32[]{:S(2)}, u32[]{:S(2)}) collective-permute-start(bf16[4,128,256]{2,1,0:T(8,128)(2,1)S(1)} %collective-permute-done.2.refs_0_), channel_id=1, source_target_pairs={{0,112},{4,116},{8,120},{12,124},{16,32},{20,36},{24,40},{28,44},{... | collective-permute-start | bytes 786440 | tf_op jit(solution)/shard_map/ppermute | solution.py:28
  61.8 4.5 %copy-start.1 = (bf16[1024,1536]{1,0:T(8,128)(2,1)S(1)}, bf16[1024,1536]{1,0:T(8,128)(2,1)}, u32[]{:S(2)}) copy-start(bf16[1024,1536]{1,0:T(8,128)(2,1)} %refs_3_.1) | copy-start | bytes 9437188

commit v4 on v3

--- a/solution.py
+++ b/solution.py
@@ -23,7 +23,7 @@
 def swap_z(x, odd):
     pairs = []
     for z in range(Z):
-        partner = (z + (1 if z % 2 == odd else -1)) % Z
+        partner = (z + (1 if z % 2 != odd else -1)) % Z
         pairs += [(z * Y + y, partner * Y + y) for y in range(Y)]
     return lax.ppermute(x, "ctx", pairs)
 
@@ -87,7 +87,7 @@
         q_all[h * rows : (h + 1) * rows, HEAD:] = eye
     me = ids[0]
     z = me // Y
-    sign = 1 - 2 * (z % 2)
+    sign = 2 * (z % 2) - 1
     row = lax.broadcasted_iota(jnp.int32, (SPAN, 2 * SPAN), 1)
     key = lax.broadcasted_iota(jnp.int32, (SPAN, 2 * SPAN), 0)
     row_pos = jnp.where(row < SPAN, order[2 * me] * SPAN + row, order[2 * me + 1] * SPAN + row - SPAN)

time: 91 us -> 90.5 us (level)
  starting transfers between devices: 39.4 us -> 37.1 us
  waiting for transfers between devices: 15.7 us -> 17.6 us
    ppermute x7, starting transfers between devices: 30.3 us -> 28 us  [swap_z(): return lax.ppermute(x, 'ctx', pairs)]
    ppermute x7, waiting for transfers between devices: 10.5 us -> 12.3 us  [swap_z(): return lax.ppermute(x, 'ctx', pairs)]
  transfers between devices with their start and end apart: 8 -> 8, of which waited for: 6 -> 7; matrix products, arithmetic and copies ran while one was open for 0% -> 0% of each run, Pallas kernels for 8% -> 8%
where the time goes in v4:
time: 90.5 us; the launch traced here: 89.9 us
  starting transfers between devices  37.1 us (41%)
  blocking collectives  19.9 us (22%)
  waiting for transfers between devices  17.6 us (19%)
  Pallas kernels  12.4 us (14%)
  local copies, waits for them, and re-layouts  1.61 us (2%)
    ppermute x7, starting transfers between devices, swap_z(): return lax.ppermute(x, 'ctx', pairs)  28 us
    ppermute x7, waiting for transfers between devices, swap_z(): return lax.ppermute(x, 'ctx', pairs)  12.3 us
    all_to_all x1, blocking collectives, body(): parts = lax.all_to_all(parts, 'tp', 0, 0, tiled=True)  11.6 us
    all_to_all x1, starting transfers between devices, body(): lax.all_to_all(pack(keys, values), 'ctx', 0, 0, axis_index_groups=Y_GROUP...  9.1 us
    all_to_all x1, blocking collectives, body(): ratio = lax.all_to_all(ratio, 'tp', 0, 0, tiled=True)  8.29 us
    pallas_call x5, Pallas kernels, attend(): pl.pallas_call(functools.partial(attend_kernel, start, len(kvs), first, l...  8.13 us
    all_to_all x1, waiting for transfers between devices, body(): lax.all_to_all(pack(keys, values), 'ctx', 0, 0, axis_index_groups=Y_GROUP...  5.25 us
    pallas_call x1, Pallas kernels, body(): pl.pallas_call(ratio_kernel, out_shape=jax.ShapeDtypeStruct((TP, 1, rows)...  1.85 us
  transfers between devices with their start and end apart: 8, of which 7 were waited for; matrix products, arithmetic and copies ran while one was open for 0% of the time, Pallas kernels for 8%

profile of v4, /device:TPU:16, one launch (start us, length us, event | category | flops | bytes accessed | tf_op | source)
XLA Modules:
  0.0 89.9 jit_solution(16254415673375930733)
XLA Ops:
  0.6 1.5 %pack.1 = bf16[4,128,256]{2,1,0:T(8,128)(2,1)} custom-call(bf16[128,128]{1,0:T(8,128)(2,1)} %k_ref.1, bf16[128,128]{1,0:T(8,128)(2,1)} %v_ref.1), custom_call_target="tpu_custom_call" | custom-call | tf_op jit(solution)/shard_map/pack/pallas_call | solution.py:62
  2.1 9.1 %all-to-all-start = ((bf16[4,128,256]{2,1,0:T(8,128)(2,1)}), bf16[4,128,256]{2,1,0:T(8,128)(2,1)S(1)}, u32[]{:S(2)}, u32[]{:S(2)}) async-start(bf16[4,128,256]{2,1,0:T(8,128)(2,1)} %pack.1), calls=%async_computation | async-start | bytes 524288 | tf_op jit(solution)/shard_map/all_to_all | solution.py:227
  11.3 0.9 %copy-done.2 = bf16[128,1024]{1,0:T(8,128)(2,1)S(1)} copy-done((bf16[128,1024]{1,0:T(8,128)(2,1)S(1)}, bf16[128,1024]{1,0:T(8,128)(2,1)}, u32[]{:S(2)}) %copy-start.2) | copy-done | bytes 262168
  13.9 5.2 %all-to-all-done.refs_0_ = bf16[4,128,256]{2,1,0:T(8,128)(2,1)S(1)} async-done(((bf16[4,128,256]{2,1,0:T(8,128)(2,1)}), bf16[4,128,256]{2,1,0:T(8,128)(2,1)S(1)}, u32[]{:S(2)}, u32[]{:S(2)}) %all-to-all-start) | async-done | bytes 262176 | tf_op jit(solution)/shard_map/all_to_all | solution.py:227
  19.1 10.9 %collective-permute-start = (bf16[4,128,256]{2,1,0:T(8,128)(2,1)S(1)}, bf16[4,128,256]{2,1,0:T(8,128)(2,1)S(1)}, u32[]{:S(2)}, u32[]{:S(2)}) collective-permute-start(bf16[4,128,256]{2,1,0:T(8,128)(2,1)S(1)} %all-to-all-done.refs_0_), channel_id=1, source_target_pairs={{0,112},{4,116},{8,120},{12,124},{16,32},{20,36},{24,40},{28,44},{... | collective-permute-start | bytes 786440 | tf_op jit(solution)/shard_map/ppermute | solution.py:28
  30.0 1.9 %collective-permute-start.4 = (bf16[4,128,256]{2,1,0:T(8,128)(2,1)S(1)}, bf16[4,128,256]{2,1,0:T(8,128)(2,1)S(1)}, u32[]{:S(2)}, u32[]{:S(2)}) collective-permute-start(bf16[4,128,256]{2,1,0:T(8,128)(2,1)S(1)} %all-to-all-done.refs_0_), channel_id=1, source_target_pairs={{0,16},{4,20},{8,24},{12,28},{16,0},{20,4},{24,8},{28,12},{32,48},... | collective-permute-start | bytes 786440 | tf_op jit(solution)/shard_map/ppermute | solution.py:28
  32.0 4.3 %collective-permute-done.refs_0_ = bf16[4,128,256]{2,1,0:T(8,128)(2,1)S(1)} collective-permute-done((bf16[4,128,256]{2,1,0:T(8,128)(2,1)S(1)}, bf16[4,128,256]{2,1,0:T(8,128)(2,1)S(1)}, u32[]{:S(2)}, u32[]{:S(2)}) %collective-permute-start) | collective-permute-done | bytes 262176 | tf_op jit(solution)/shard_map/ppermute | solution.py:28
  36.3 1.9 %collective-permute-start.1 = (bf16[4,128,256]{2,1,0:T(8,128)(2,1)S(1)}, bf16[4,128,256]{2,1,0:T(8,128)(2,1)S(1)}, u32[]{:S(2)}, u32[]{:S(2)}) collective-permute-start(bf16[4,128,256]{2,1,0:T(8,128)(2,1)S(1)} %collective-permute-done.refs_0_), channel_id=1, source_target_pairs={{0,16},{4,20},{8,24},{12,28},{16,0},{20,4},{24,8},{28,12},{32,48},... | collective-permute-start | bytes 786440 | tf_op jit(solution)/shard_map/ppermute | solution.py:28
  38.2 1.0 %attend.4 = (f32[1024,256]{1,0:T(8,128)S(1)}, f32[1024,128]{1,0:T(8,128)S(1)}) custom-call(bf16[1024,256]{1,0:T(8,128)(2,1)S(1)} %get-tuple-element.26.q_all, bf16[4096,128]{1,0:T(8,128)(2,1)S(1)} %get-tuple-element.27.bias_ref, bf16[4,128,256]{2,1,0:T(8,128)(2,1)S(1)} %all-to-all-done.refs_0_), custom_call_target="tpu_custom_call" | custom-call | flops 2147483648 | bytes 4194304 | tf_op jit(solution)/shard_map/attend/pallas_call | solution.py:187
  39.6 4.4 %collective-permute-start.5 = (bf16[4,128,256]{2,1,0:T(8,128)(2,1)S(1)}, bf16[4,128,256]{2,1,0:T(8,128)(2,1)S(1)}, u32[]{:S(2)}, u32[]{:S(2)}) collective-permute-start(bf16[4,128,256]{2,1,0:T(8,128)(2,1)S(1)} %collective-permute-done.4.refs_1_), channel_id=1, source_target_pairs={{0,112},{4,116},{8,120},{12,124},{16,32},{20,36},{24,40},{28,44},{... | collective-permute-start | bytes 786440 | tf_op jit(solution)/shard_map/ppermute | solution.py:28
  44.0 1.5 %collective-permute-done.1.refs_0_ = bf16[4,128,256]{2,1,0:T(8,128)(2,1)S(1)} collective-permute-done((bf16[4,128,256]{2,1,0:T(8,128)(2,1)S(1)}, bf16[4,128,256]{2,1,0:T(8,128)(2,1)S(1)}, u32[]{:S(2)}, u32[]{:S(2)}) %collective-permute-start.1) | collective-permute-done | bytes 262176 | tf_op jit(solution)/shard_map/ppermute | solution.py:28
  45.6 4.5 %collective-permute-start.2 = (bf16[4,128,256]{2,1,0:T(8,128)(2,1)S(1)}, bf16[4,128,256]{2,1,0:T(8,128)(2,1)S(1)}, u32[]{:S(2)}, u32[]{:S(2)}) collective-permute-start(bf16[4,128,256]{2,1,0:T(8,128)(2,1)S(1)} %collective-permute-done.1.refs_0_), channel_id=1, source_target_pairs={{0,112},{4,116},{8,120},{12,124},{16,32},{20,36},{24,40},{28,44},{... | collective-permute-start | bytes 786440 | tf_op jit(solution)/shard_map/ppermute | solution.py:28
  50.1 1.8 %attend.5 = (f32[1024,256]{1,0:T(8,128)S(1)}, f32[1024,128]{1,0:T(8,128)S(1)}) custom-call(bf16[1024,256]{1,0:T(8,128)(2,1)S(1)} %get-tuple-element.26.q_all, bf16[4096,128]{1,0:T(8,128)(2,1)S(1)} %get-tuple-element.27.bias_ref, bf16[4,128,256]{2,1,0:T(8,128)(2,1)S(1)} %collective-permute-done.refs_0_, ...), custom_call_target="tpu_custom_call" | custom-call | flops 4294967296 | bytes 4194304 | tf_op jit(solution)/shard_map/attend/pallas_call | solution.py:187
  51.9 1.9 %collective-permute-start.6 = (bf16[4,128,256]{2,1,0:T(8,128)(2,1)S(1)}, bf16[4,128,256]{2,1,0:T(8,128)(2,1)S(1)}, u32[]{:S(2)}, u32[]{:S(2)}) collective-permute-start(bf16[4,128,256]{2,1,0:T(8,128)(2,1)S(1)} %collective-permute-done.5.refs_1_), channel_id=1, source_target_pairs={{0,16},{4,20},{8,24},{12,28},{16,0},{20,4},{24,8},{28,12},{32,48},... | collective-permute-start | bytes 786440 | tf_op jit(solution)/shard_map/ppermute | solution.py:28
  53.8 1.5 %collective-permute-done.2.refs_0_ = bf16[4,128,256]{2,1,0:T(8,128)(2,1)S(1)} collective-permute-done((bf16[4,128,256]{2,1,0:T(8,128)(2,1)S(1)}, bf16[4,128,256]{2,1,0:T(8,128)(2,1)S(1)}, u32[]{:S(2)}, u32[]{:S(2)}) %collective-permute-start.2) | collective-permute-done | bytes 262176 | tf_op jit(solution)/shard_map/ppermute | solution.py:28
  55.3 2.4 %collective-permute-start.3 = (bf16[4,128,256]{2,1,0:T(8,128)(2,1)S(1)}, bf16[4,128,256]{2,1,0:T(8,128)(2,1)S(1)}, u32[]{:S(2)}, u32[]{:S(2)}) collective-permute-start(bf16[4,128,256]{2,1,0:T(8,128)(2,1)S(1)} %collective-permute-done.2.refs_0_), channel_id=1, source_target_pairs={{0,16},{4,20},{8,24},{12,28},{16,0},{20,4},{24,8},{28,12},{32,48},... | collective-permute-start | bytes 786440 | tf_op jit(solution)/shard_map/ppermute | solution.py:28
  57.7 1.8 %attend.6 = (f32[1024,256]{1,0:T(8,128)S(1)}, f32[1024,128]{1,0:T(8,128)S(1)}) custom-call(bf16[1024,256]{1,0:T(8,128)(2,1)S(1)} %get-tuple-element.26.q_all, bf16[4096,128]{1,0:T(8,128)(2,1)S(1)} %get-tuple-element.27.bias_ref, bf16[4,128,256]{2,1,0:T(8,128)(2,1)S(1)} %collective-permute-done.1.refs_0_, ...), custom_call_target="tpu_custom_call" | custom-call | flops 4294967296 | bytes 4194304 | tf_op jit(solution)/shard_map/attend/pallas_call | solution.py:187
  59.5 3.3 %collective-permute-done.6.refs_1_ = bf16[4,128,256]{2,1,0:T(8,128)(2,1)S(1)} collective-permute-done((bf16[4,128,256]{2,1,0:T(8,128)(2,1)S(1)}, bf16[4,128,256]{2,1,0:T(8,128)(2,1)S(1)}, u32[]{:S(2)}, u32[]{:S(2)}) %collective-permute-start.6) | collective-permute-done | bytes 262176 | tf_op jit(solution)/shard_map/ppermute | solution.py:28
  62.8 1.8 %attend.7 = (f32[1024,256]{1,0:T(8,128)S(1)}, f32[1024,128]{1,0:T(8,128)S(1)}) custom-call(bf16[1024,256]{1,0:T(8,128)(2,1)S(1)} %get-tuple-element.26.q_all, bf16[4096,128]{1,0:T(8,128)(2,1)S(1)} %get-tuple-element.27.bias_ref, bf16[4,128,256]{2,1,0:T(8,128)(2,1)S(1)} %collective-permute-done.2.refs_0_, ...), custom_call_target="tpu_custom_call" | custom-call | flops 4294967296 | bytes 4194304 | tf_op jit(solution)/shard_map/attend/pallas_call | solution.py:187
  64.6 1.2 %collective-permute-done.3.refs_0_ = bf16[4,128,256]{2,1,0:T(8,128)(2,1)S(1)} collective-permute-done((bf16[4,128,256]{2,1,0:T(8,128)(2,1)S(1)}, bf16[4,128,256]{2,1,0:T(8,128)(2,1)S(1)}, u32[]{:S(2)}, u32[]{:S(2)}) %collective-permute-start.3) | collective-permute-done | bytes 262176 | tf_op jit(solution)/shard_map/ppermute | solution.py:28
  65.8 1.9 %attend_last.1 = (bf16[128,1024]{1,0:T(8,128)(2,1)}, bf16[4,32,1536]{2,1,0:T(8,128)(2,1)S(1)}) custom-call(bf16[1024,256]{1,0:T(8,128)(2,1)S(1)} %get-tuple-element.26.q_all, bf16[4096,128]{1,0:T(8,128)(2,1)S(1)} %get-tuple-element.27.bias_ref, bf16[4,128,256]{2,1,0:T(8,128)(2,1)S(1)} %collective-permute-done.3.refs_0_, ...), custom_call_target="tpu_custom_call" | custom-call | flops 2147483648 | bytes 4194304 | tf_op jit(solution)/shard_map/attend_last/pallas_call | solution.py:187
  67.7 11.6 %all_to_all.15.part_ref = bf16[4,32,1536]{2,1,0:T(8,128)(2,1)} all-to-all(bf16[4,32,1536]{2,1,0:T(8,128)(2,1)S(1)} %get-tuple-element.45), channel_id=1, replica_groups=mesh['dp'=4,'ctx'=32,'tp'=4] {'tp'}, dimensions={0} | all-to-all | bytes 786432 | tf_op jit(solution)/shard_map/all_to_all | solution.py:244
  79.2 1.9 %ratio.1 = f32[4,1,128]{2,1,0:T(1,128)} custom-call(s32[2]{0:T(128)} %copy-done, bf16[4,32,1536]{2,1,0:T(8,128)(2,1)} %all_to_all.15.part_ref, s32[1,128]{1,0:T(1,128)} %bitcast.4, f32[1,128]{1,0:T(1,128)} %bitcast.5), custom_call_target="tpu_custom_call" | custom-call | tf_op jit(solution)/shard_map/ratio/pallas_call | solution.py:246
  81.1 8.3 %all_to_all.16 = f32[4,1,128]{2,1,0:T(1,128)S(1)} all-to-all(f32[4,1,128]{2,1,0:T(1,128)} %ratio.1), channel_id=1, replica_groups=mesh['dp'=4,'ctx'=32,'tp'=4] {'tp'}, dimensions={0} | all-to-all | bytes 4096 | tf_op jit(solution)/shard_map/all_to_all | solution.py:253
  (12 shorter events, 2.7 us)
Async XLA Ops:
  2.1 17.0 %all-to-all-start = ((bf16[4,128,256]{2,1,0:T(8,128)(2,1)}), bf16[4,128,256]{2,1,0:T(8,128)(2,1)S(1)}, u32[]{:S(2)}, u32[]{:S(2)}) async-start(bf16[4,128,256]{2,1,0:T(8,128)(2,1)} %pack.1), calls=%async_computation | async-start | bytes 524288 | tf_op jit(solution)/shard_map/all_to_all | solution.py:227
  11.3 0.9 %copy-start.2 = (bf16[128,1024]{1,0:T(8,128)(2,1)S(1)}, bf16[128,1024]{1,0:T(8,128)(2,1)}, u32[]{:S(2)}) copy-start(bf16[128,1024]{1,0:T(8,128)(2,1)} %q_ref.1) | copy-start | bytes 786436
  12.3 0.7 copy-start.3
  12.9 0.9 %copy-start = (s32[2]{0:T(128)}, s32[2]{0:T(128)S(1)}, u32[]{:S(2)}) copy-start(s32[2]{0:T(128)S(1)} %pad_add_fusion.ids) | copy-start | bytes 28
  19.1 17.2 %collective-permute-start = (bf16[4,128,256]{2,1,0:T(8,128)(2,1)S(1)}, bf16[4,128,256]{2,1,0:T(8,128)(2,1)S(1)}, u32[]{:S(2)}, u32[]{:S(2)}) collective-permute-start(bf16[4,128,256]{2,1,0:T(8,128)(2,1)S(1)} %all-to-all-done.refs_0_), channel_id=1, source_target_pairs={{0,112},{4,116},{8,120},{12,124},{16,32},{20,36},{24,40},{28,44},{... | collective-permute-start | bytes 786440 | tf_op jit(solution)/shard_map/ppermute | solution.py:28
  30.0 9.6 %collective-permute-start.4 = (bf16[4,128,256]{2,1,0:T(8,128)(2,1)S(1)}, bf16[4,128,256]{2,1,0:T(8,128)(2,1)S(1)}, u32[]{:S(2)}, u32[]{:S(2)}) collective-permute-start(bf16[4,128,256]{2,1,0:T(8,128)(2,1)S(1)} %all-to-all-done.refs_0_), channel_id=1, source_target_pairs={{0,16},{4,20},{8,24},{12,28},{16,0},{20,4},{24,8},{28,12},{32,48},... | collective-permute-start | bytes 786440 | tf_op jit(solution)/shard_map/ppermute | solution.py:28
  36.3 9.3 %collective-permute-start.1 = (bf16[4,128,256]{2,1,0:T(8,128)(2,1)S(1)}, bf16[4,128,256]{2,1,0:T(8,128)(2,1)S(1)}, u32[]{:S(2)}, u32[]{:S(2)}) collective-permute-start(bf16[4,128,256]{2,1,0:T(8,128)(2,1)S(1)} %collective-permute-done.refs_0_), channel_id=1, source_target_pairs={{0,16},{4,20},{8,24},{12,28},{16,0},{20,4},{24,8},{28,12},{32,48},... | collective-permute-start | bytes 786440 | tf_op jit(solution)/shard_map/ppermute | solution.py:28
  39.6 12.2 %collective-permute-start.5 = (bf16[4,128,256]{2,1,0:T(8,128)(2,1)S(1)}, bf16[4,128,256]{2,1,0:T(8,128)(2,1)S(1)}, u32[]{:S(2)}, u32[]{:S(2)}) collective-permute-start(bf16[4,128,256]{2,1,0:T(8,128)(2,1)S(1)} %collective-permute-done.4.refs_1_), channel_id=1, source_target_pairs={{0,112},{4,116},{8,120},{12,124},{16,32},{20,36},{24,40},{28,44},{... | collective-permute-start | bytes 786440 | tf_op jit(solution)/shard_map/ppermute | solution.py:28
  45.6 9.7 %collective-permute-start.2 = (bf16[4,128,256]{2,1,0:T(8,128)(2,1)S(1)}, bf16[4,128,256]{2,1,0:T(8,128)(2,1)S(1)}, u32[]{:S(2)}, u32[]{:S(2)}) collective-permute-start(bf16[4,128,256]{2,1,0:T(8,128)(2,1)S(1)} %collective-permute-done.1.refs_0_), channel_id=1, source_target_pairs={{0,112},{4,116},{8,120},{12,124},{16,32},{20,36},{24,40},{28,44},{... | collective-permute-start | bytes 786440 | tf_op jit(solution)/shard_map/ppermute | solution.py:28
  51.9 11.0 %collective-permute-start.6 = (bf16[4,128,256]{2,1,0:T(8,128)(2,1)S(1)}, bf16[4,128,256]{2,1,0:T(8,128)(2,1)S(1)}, u32[]{:S(2)}, u32[]{:S(2)}) collective-permute-start(bf16[4,128,256]{2,1,0:T(8,128)(2,1)S(1)} %collective-permute-done.5.refs_1_), channel_id=1, source_target_pairs={{0,16},{4,20},{8,24},{12,28},{16,0},{20,4},{24,8},{28,12},{32,48},... | collective-permute-start | bytes 786440 | tf_op jit(solution)/shard_map/ppermute | solution.py:28
  55.3 10.4 %collective-permute-start.3 = (bf16[4,128,256]{2,1,0:T(8,128)(2,1)S(1)}, bf16[4,128,256]{2,1,0:T(8,128)(2,1)S(1)}, u32[]{:S(2)}, u32[]{:S(2)}) collective-permute-start(bf16[4,128,256]{2,1,0:T(8,128)(2,1)S(1)} %collective-permute-done.2.refs_0_), channel_id=1, source_target_pairs={{0,16},{4,20},{8,24},{12,28},{16,0},{20,4},{24,8},{28,12},{32,48},... | collective-permute-start | bytes 786440 | tf_op jit(solution)/shard_map/ppermute | solution.py:28
  62.8 2.9 %copy-start.1 = (bf16[1024,1536]{1,0:T(8,128)(2,1)S(1)}, bf16[1024,1536]{1,0:T(8,128)(2,1)}, u32[]{:S(2)}) copy-start(bf16[1024,1536]{1,0:T(8,128)(2,1)} %refs_3_.1) | copy-start | bytes 9437188

commit v5 on v4

--- a/solution.py
+++ b/solution.py
@@ -13,7 +13,7 @@
 Y = 4
 TP = 4
 SPAN = 64
-ROW_TILE = 256
+ROW_TILE = 512
 EXP2_SCALE = math.log2(math.e) / math.sqrt(HEAD)
 MASKED = -1e30
 COST = 4

time: 90.5 us -> 90.6 us (level)
  no operation moved by 1% of the time
where the time goes in v5:
time: 90.6 us; the launch traced here: 90 us
  starting transfers between devices  37.2 us (41%)
  blocking collectives  19.9 us (22%)
  waiting for transfers between devices  17.3 us (19%)
  Pallas kernels  12.7 us (14%)
  local copies, waits for them, and re-layouts  1.61 us (2%)
    ppermute x7, starting transfers between devices, swap_z(): return lax.ppermute(x, 'ctx', pairs)  28.1 us
    ppermute x7, waiting for transfers between devices, swap_z(): return lax.ppermute(x, 'ctx', pairs)  12 us
    all_to_all x1, blocking collectives, body(): parts = lax.all_to_all(parts, 'tp', 0, 0, tiled=True)  11.6 us
    all_to_all x1, starting transfers between devices, body(): lax.all_to_all(pack(keys, values), 'ctx', 0, 0, axis_index_groups=Y_GROUP...  9.1 us
    pallas_call x5, Pallas kernels, attend(): pl.pallas_call(functools.partial(attend_kernel, start, len(kvs), first, l...  8.38 us
    all_to_all x1, blocking collectives, body(): ratio = lax.all_to_all(ratio, 'tp', 0, 0, tiled=True)  8.29 us
    all_to_all x1, waiting for transfers between devices, body(): lax.all_to_all(pack(keys, values), 'ctx', 0, 0, axis_index_groups=Y_GROUP...  5.25 us
    pallas_call x1, Pallas kernels, body(): pl.pallas_call(ratio_kernel, out_shape=jax.ShapeDtypeStruct((TP, 1, rows)...  1.85 us
  transfers between devices with their start and end apart: 8, of which 7 were waited for; matrix products, arithmetic and copies ran while one was open for 0% of the time, Pallas kernels for 8%

profile of v5, /device:TPU:16, one launch (start us, length us, event | category | flops | bytes accessed | tf_op | source)
XLA Modules:
  0.0 90.0 jit_solution(5829170821102528503)
XLA Ops:
  0.6 1.5 %pack.1 = bf16[4,128,256]{2,1,0:T(8,128)(2,1)} custom-call(bf16[128,128]{1,0:T(8,128)(2,1)} %k_ref.1, bf16[128,128]{1,0:T(8,128)(2,1)} %v_ref.1), custom_call_target="tpu_custom_call" | custom-call | tf_op jit(solution)/shard_map/pack/pallas_call | solution.py:62
  2.1 9.1 %all-to-all-start = ((bf16[4,128,256]{2,1,0:T(8,128)(2,1)}), bf16[4,128,256]{2,1,0:T(8,128)(2,1)S(1)}, u32[]{:S(2)}, u32[]{:S(2)}) async-start(bf16[4,128,256]{2,1,0:T(8,128)(2,1)} %pack.1), calls=%async_computation | async-start | bytes 524288 | tf_op jit(solution)/shard_map/all_to_all | solution.py:227
  11.3 0.9 %copy-done.2 = bf16[128,1024]{1,0:T(8,128)(2,1)S(1)} copy-done((bf16[128,1024]{1,0:T(8,128)(2,1)S(1)}, bf16[128,1024]{1,0:T(8,128)(2,1)}, u32[]{:S(2)}) %copy-start.2) | copy-done | bytes 262168
  13.9 5.2 %all-to-all-done.refs_0_ = bf16[4,128,256]{2,1,0:T(8,128)(2,1)S(1)} async-done(((bf16[4,128,256]{2,1,0:T(8,128)(2,1)}), bf16[4,128,256]{2,1,0:T(8,128)(2,1)S(1)}, u32[]{:S(2)}, u32[]{:S(2)}) %all-to-all-start) | async-done | bytes 262176 | tf_op jit(solution)/shard_map/all_to_all | solution.py:227
  19.1 10.9 %collective-permute-start = (bf16[4,128,256]{2,1,0:T(8,128)(2,1)S(1)}, bf16[4,128,256]{2,1,0:T(8,128)(2,1)S(1)}, u32[]{:S(2)}, u32[]{:S(2)}) collective-permute-start(bf16[4,128,256]{2,1,0:T(8,128)(2,1)S(1)} %all-to-all-done.refs_0_), channel_id=1, source_target_pairs={{0,112},{4,116},{8,120},{12,124},{16,32},{20,36},{24,40},{28,44},{... | collective-permute-start | bytes 786440 | tf_op jit(solution)/shard_map/ppermute | solution.py:28
  30.0 1.9 %collective-permute-start.4 = (bf16[4,128,256]{2,1,0:T(8,128)(2,1)S(1)}, bf16[4,128,256]{2,1,0:T(8,128)(2,1)S(1)}, u32[]{:S(2)}, u32[]{:S(2)}) collective-permute-start(bf16[4,128,256]{2,1,0:T(8,128)(2,1)S(1)} %all-to-all-done.refs_0_), channel_id=1, source_target_pairs={{0,16},{4,20},{8,24},{12,28},{16,0},{20,4},{24,8},{28,12},{32,48},... | collective-permute-start | bytes 786440 | tf_op jit(solution)/shard_map/ppermute | solution.py:28
  32.0 4.3 %collective-permute-done.refs_0_ = bf16[4,128,256]{2,1,0:T(8,128)(2,1)S(1)} collective-permute-done((bf16[4,128,256]{2,1,0:T(8,128)(2,1)S(1)}, bf16[4,128,256]{2,1,0:T(8,128)(2,1)S(1)}, u32[]{:S(2)}, u32[]{:S(2)}) %collective-permute-start) | collective-permute-done | bytes 262176 | tf_op jit(solution)/shard_map/ppermute | solution.py:28
  36.3 1.9 %collective-permute-start.1 = (bf16[4,128,256]{2,1,0:T(8,128)(2,1)S(1)}, bf16[4,128,256]{2,1,0:T(8,128)(2,1)S(1)}, u32[]{:S(2)}, u32[]{:S(2)}) collective-permute-start(bf16[4,128,256]{2,1,0:T(8,128)(2,1)S(1)} %collective-permute-done.refs_0_), channel_id=1, source_target_pairs={{0,16},{4,20},{8,24},{12,28},{16,0},{20,4},{24,8},{28,12},{32,48},... | collective-permute-start | bytes 786440 | tf_op jit(solution)/shard_map/ppermute | solution.py:28
  38.2 0.9 %attend.4 = (f32[1024,256]{1,0:T(8,128)S(1)}, f32[1024,128]{1,0:T(8,128)S(1)}) custom-call(bf16[1024,256]{1,0:T(8,128)(2,1)S(1)} %get-tuple-element.26.q_all, bf16[4096,128]{1,0:T(8,128)(2,1)S(1)} %get-tuple-element.27.bias_ref, bf16[4,128,256]{2,1,0:T(8,128)(2,1)S(1)} %all-to-all-done.refs_0_), custom_call_target="tpu_custom_call" | custom-call | flops 2147483648 | bytes 4194304 | tf_op jit(solution)/shard_map/attend/pallas_call | solution.py:187
  39.6 4.4 %collective-permute-start.5 = (bf16[4,128,256]{2,1,0:T(8,128)(2,1)S(1)}, bf16[4,128,256]{2,1,0:T(8,128)(2,1)S(1)}, u32[]{:S(2)}, u32[]{:S(2)}) collective-permute-start(bf16[4,128,256]{2,1,0:T(8,128)(2,1)S(1)} %collective-permute-done.4.refs_1_), channel_id=1, source_target_pairs={{0,112},{4,116},{8,120},{12,124},{16,32},{20,36},{24,40},{28,44},{... | collective-permute-start | bytes 786440 | tf_op jit(solution)/shard_map/ppermute | solution.py:28
  44.0 1.6 %collective-permute-done.1.refs_0_ = bf16[4,128,256]{2,1,0:T(8,128)(2,1)S(1)} collective-permute-done((bf16[4,128,256]{2,1,0:T(8,128)(2,1)S(1)}, bf16[4,128,256]{2,1,0:T(8,128)(2,1)S(1)}, u32[]{:S(2)}, u32[]{:S(2)}) %collective-permute-start.1) | collective-permute-done | bytes 262176 | tf_op jit(solution)/shard_map/ppermute | solution.py:28
  45.6 4.5 %collective-permute-start.2 = (bf16[4,128,256]{2,1,0:T(8,128)(2,1)S(1)}, bf16[4,128,256]{2,1,0:T(8,128)(2,1)S(1)}, u32[]{:S(2)}, u32[]{:S(2)}) collective-permute-start(bf16[4,128,256]{2,1,0:T(8,128)(2,1)S(1)} %collective-permute-done.1.refs_0_), channel_id=1, source_target_pairs={{0,112},{4,116},{8,120},{12,124},{16,32},{20,36},{24,40},{28,44},{... | collective-permute-start | bytes 786440 | tf_op jit(solution)/shard_map/ppermute | solution.py:28
  50.1 1.9 %attend.5 = (f32[1024,256]{1,0:T(8,128)S(1)}, f32[1024,128]{1,0:T(8,128)S(1)}) custom-call(bf16[1024,256]{1,0:T(8,128)(2,1)S(1)} %get-tuple-element.26.q_all, bf16[4096,128]{1,0:T(8,128)(2,1)S(1)} %get-tuple-element.27.bias_ref, bf16[4,128,256]{2,1,0:T(8,128)(2,1)S(1)} %collective-permute-done.refs_0_, ...), custom_call_target="tpu_custom_call" | custom-call | flops 4294967296 | bytes 4194304 | tf_op jit(solution)/shard_map/attend/pallas_call | solution.py:187
  52.0 1.9 %collective-permute-start.6 = (bf16[4,128,256]{2,1,0:T(8,128)(2,1)S(1)}, bf16[4,128,256]{2,1,0:T(8,128)(2,1)S(1)}, u32[]{:S(2)}, u32[]{:S(2)}) collective-permute-start(bf16[4,128,256]{2,1,0:T(8,128)(2,1)S(1)} %collective-permute-done.5.refs_1_), channel_id=1, source_target_pairs={{0,16},{4,20},{8,24},{12,28},{16,0},{20,4},{24,8},{28,12},{32,48},... | collective-permute-start | bytes 786440 | tf_op jit(solution)/shard_map/ppermute | solution.py:28
  53.9 1.4 %collective-permute-done.2.refs_0_ = bf16[4,128,256]{2,1,0:T(8,128)(2,1)S(1)} collective-permute-done((bf16[4,128,256]{2,1,0:T(8,128)(2,1)S(1)}, bf16[4,128,256]{2,1,0:T(8,128)(2,1)S(1)}, u32[]{:S(2)}, u32[]{:S(2)}) %collective-permute-start.2) | collective-permute-done | bytes 262176 | tf_op jit(solution)/shard_map/ppermute | solution.py:28
  55.3 2.5 %collective-permute-start.3 = (bf16[4,128,256]{2,1,0:T(8,128)(2,1)S(1)}, bf16[4,128,256]{2,1,0:T(8,128)(2,1)S(1)}, u32[]{:S(2)}, u32[]{:S(2)}) collective-permute-start(bf16[4,128,256]{2,1,0:T(8,128)(2,1)S(1)} %collective-permute-done.2.refs_0_), channel_id=1, source_target_pairs={{0,16},{4,20},{8,24},{12,28},{16,0},{20,4},{24,8},{28,12},{32,48},... | collective-permute-start | bytes 786440 | tf_op jit(solution)/shard_map/ppermute | solution.py:28
  57.8 1.9 %attend.6 = (f32[1024,256]{1,0:T(8,128)S(1)}, f32[1024,128]{1,0:T(8,128)S(1)}) custom-call(bf16[1024,256]{1,0:T(8,128)(2,1)S(1)} %get-tuple-element.26.q_all, bf16[4096,128]{1,0:T(8,128)(2,1)S(1)} %get-tuple-element.27.bias_ref, bf16[4,128,256]{2,1,0:T(8,128)(2,1)S(1)} %collective-permute-done.1.refs_0_, ...), custom_call_target="tpu_custom_call" | custom-call | flops 4294967296 | bytes 4194304 | tf_op jit(solution)/shard_map/attend/pallas_call | solution.py:187
  59.7 3.3 %collective-permute-done.6.refs_1_ = bf16[4,128,256]{2,1,0:T(8,128)(2,1)S(1)} collective-permute-done((bf16[4,128,256]{2,1,0:T(8,128)(2,1)S(1)}, bf16[4,128,256]{2,1,0:T(8,128)(2,1)S(1)}, u32[]{:S(2)}, u32[]{:S(2)}) %collective-permute-start.6) | collective-permute-done | bytes 262176 | tf_op jit(solution)/shard_map/ppermute | solution.py:28
  63.0 1.8 %attend.7 = (f32[1024,256]{1,0:T(8,128)S(1)}, f32[1024,128]{1,0:T(8,128)S(1)}) custom-call(bf16[1024,256]{1,0:T(8,128)(2,1)S(1)} %get-tuple-element.26.q_all, bf16[4096,128]{1,0:T(8,128)(2,1)S(1)} %get-tuple-element.27.bias_ref, bf16[4,128,256]{2,1,0:T(8,128)(2,1)S(1)} %collective-permute-done.2.refs_0_, ...), custom_call_target="tpu_custom_call" | custom-call | flops 4294967296 | bytes 4194304 | tf_op jit(solution)/shard_map/attend/pallas_call | solution.py:187
  64.9 1.0 %collective-permute-done.3.refs_0_ = bf16[4,128,256]{2,1,0:T(8,128)(2,1)S(1)} collective-permute-done((bf16[4,128,256]{2,1,0:T(8,128)(2,1)S(1)}, bf16[4,128,256]{2,1,0:T(8,128)(2,1)S(1)}, u32[]{:S(2)}, u32[]{:S(2)}) %collective-permute-start.3) | collective-permute-done | bytes 262176 | tf_op jit(solution)/shard_map/ppermute | solution.py:28
  65.9 1.9 %attend_last.1 = (bf16[128,1024]{1,0:T(8,128)(2,1)}, bf16[4,32,1536]{2,1,0:T(8,128)(2,1)S(1)}) custom-call(bf16[1024,256]{1,0:T(8,128)(2,1)S(1)} %get-tuple-element.26.q_all, bf16[4096,128]{1,0:T(8,128)(2,1)S(1)} %get-tuple-element.27.bias_ref, bf16[4,128,256]{2,1,0:T(8,128)(2,1)S(1)} %collective-permute-done.3.refs_0_, ...), custom_call_target="tpu_custom_call" | custom-call | flops 2147483648 | bytes 4194304 | tf_op jit(solution)/shard_map/attend_last/pallas_call | solution.py:187
  67.7 11.6 %all_to_all.15.part_ref = bf16[4,32,1536]{2,1,0:T(8,128)(2,1)} all-to-all(bf16[4,32,1536]{2,1,0:T(8,128)(2,1)S(1)} %get-tuple-element.45), channel_id=1, replica_groups=mesh['dp'=4,'ctx'=32,'tp'=4] {'tp'}, dimensions={0} | all-to-all | bytes 786432 | tf_op jit(solution)/shard_map/all_to_all | solution.py:244
  79.3 1.9 %ratio.1 = f32[4,1,128]{2,1,0:T(1,128)} custom-call(s32[2]{0:T(128)} %copy-done, bf16[4,32,1536]{2,1,0:T(8,128)(2,1)} %all_to_all.15.part_ref, s32[1,128]{1,0:T(1,128)} %bitcast.4, f32[1,128]{1,0:T(1,128)} %bitcast.5), custom_call_target="tpu_custom_call" | custom-call | tf_op jit(solution)/shard_map/ratio/pallas_call | solution.py:246
  81.2 8.3 %all_to_all.16 = f32[4,1,128]{2,1,0:T(1,128)S(1)} all-to-all(f32[4,1,128]{2,1,0:T(1,128)} %ratio.1), channel_id=1, replica_groups=mesh['dp'=4,'ctx'=32,'tp'=4] {'tp'}, dimensions={0} | all-to-all | bytes 4096 | tf_op jit(solution)/shard_map/all_to_all | solution.py:253
  (12 shorter events, 2.7 us)
Async XLA Ops:
  2.1 17.0 %all-to-all-start = ((bf16[4,128,256]{2,1,0:T(8,128)(2,1)}), bf16[4,128,256]{2,1,0:T(8,128)(2,1)S(1)}, u32[]{:S(2)}, u32[]{:S(2)}) async-start(bf16[4,128,256]{2,1,0:T(8,128)(2,1)} %pack.1), calls=%async_computation | async-start | bytes 524288 | tf_op jit(solution)/shard_map/all_to_all | solution.py:227
  11.3 0.9 %copy-start.2 = (bf16[128,1024]{1,0:T(8,128)(2,1)S(1)}, bf16[128,1024]{1,0:T(8,128)(2,1)}, u32[]{:S(2)}) copy-start(bf16[128,1024]{1,0:T(8,128)(2,1)} %q_ref.1) | copy-start | bytes 786436
  12.3 0.7 copy-start.3
  12.9 0.9 %copy-start = (s32[2]{0:T(128)}, s32[2]{0:T(128)S(1)}, u32[]{:S(2)}) copy-start(s32[2]{0:T(128)S(1)} %pad_add_fusion.ids) | copy-start | bytes 28
  19.1 17.2 %collective-permute-start = (bf16[4,128,256]{2,1,0:T(8,128)(2,1)S(1)}, bf16[4,128,256]{2,1,0:T(8,128)(2,1)S(1)}, u32[]{:S(2)}, u32[]{:S(2)}) collective-permute-start(bf16[4,128,256]{2,1,0:T(8,128)(2,1)S(1)} %all-to-all-done.refs_0_), channel_id=1, source_target_pairs={{0,112},{4,116},{8,120},{12,124},{16,32},{20,36},{24,40},{28,44},{... | collective-permute-start | bytes 786440 | tf_op jit(solution)/shard_map/ppermute | solution.py:28
  30.0 9.6 %collective-permute-start.4 = (bf16[4,128,256]{2,1,0:T(8,128)(2,1)S(1)}, bf16[4,128,256]{2,1,0:T(8,128)(2,1)S(1)}, u32[]{:S(2)}, u32[]{:S(2)}) collective-permute-start(bf16[4,128,256]{2,1,0:T(8,128)(2,1)S(1)} %all-to-all-done.refs_0_), channel_id=1, source_target_pairs={{0,16},{4,20},{8,24},{12,28},{16,0},{20,4},{24,8},{28,12},{32,48},... | collective-permute-start | bytes 786440 | tf_op jit(solution)/shard_map/ppermute | solution.py:28
  36.3 9.3 %collective-permute-start.1 = (bf16[4,128,256]{2,1,0:T(8,128)(2,1)S(1)}, bf16[4,128,256]{2,1,0:T(8,128)(2,1)S(1)}, u32[]{:S(2)}, u32[]{:S(2)}) collective-permute-start(bf16[4,128,256]{2,1,0:T(8,128)(2,1)S(1)} %collective-permute-done.refs_0_), channel_id=1, source_target_pairs={{0,16},{4,20},{8,24},{12,28},{16,0},{20,4},{24,8},{28,12},{32,48},... | collective-permute-start | bytes 786440 | tf_op jit(solution)/shard_map/ppermute | solution.py:28
  39.6 12.3 %collective-permute-start.5 = (bf16[4,128,256]{2,1,0:T(8,128)(2,1)S(1)}, bf16[4,128,256]{2,1,0:T(8,128)(2,1)S(1)}, u32[]{:S(2)}, u32[]{:S(2)}) collective-permute-start(bf16[4,128,256]{2,1,0:T(8,128)(2,1)S(1)} %collective-permute-done.4.refs_1_), channel_id=1, source_target_pairs={{0,112},{4,116},{8,120},{12,124},{16,32},{20,36},{24,40},{28,44},{... | collective-permute-start | bytes 786440 | tf_op jit(solution)/shard_map/ppermute | solution.py:28
  45.6 9.7 %collective-permute-start.2 = (bf16[4,128,256]{2,1,0:T(8,128)(2,1)S(1)}, bf16[4,128,256]{2,1,0:T(8,128)(2,1)S(1)}, u32[]{:S(2)}, u32[]{:S(2)}) collective-permute-start(bf16[4,128,256]{2,1,0:T(8,128)(2,1)S(1)} %collective-permute-done.1.refs_0_), channel_id=1, source_target_pairs={{0,112},{4,116},{8,120},{12,124},{16,32},{20,36},{24,40},{28,44},{... | collective-permute-start | bytes 786440 | tf_op jit(solution)/shard_map/ppermute | solution.py:28
  52.0 11.1 %collective-permute-start.6 = (bf16[4,128,256]{2,1,0:T(8,128)(2,1)S(1)}, bf16[4,128,256]{2,1,0:T(8,128)(2,1)S(1)}, u32[]{:S(2)}, u32[]{:S(2)}) collective-permute-start(bf16[4,128,256]{2,1,0:T(8,128)(2,1)S(1)} %collective-permute-done.5.refs_1_), channel_id=1, source_target_pairs={{0,16},{4,20},{8,24},{12,28},{16,0},{20,4},{24,8},{28,12},{32,48},... | collective-permute-start | bytes 786440 | tf_op jit(solution)/shard_map/ppermute | solution.py:28
  55.3 10.6 %collective-permute-start.3 = (bf16[4,128,256]{2,1,0:T(8,128)(2,1)S(1)}, bf16[4,128,256]{2,1,0:T(8,128)(2,1)S(1)}, u32[]{:S(2)}, u32[]{:S(2)}) collective-permute-start(bf16[4,128,256]{2,1,0:T(8,128)(2,1)S(1)} %collective-permute-done.2.refs_0_), channel_id=1, source_target_pairs={{0,16},{4,20},{8,24},{12,28},{16,0},{20,4},{24,8},{28,12},{32,48},... | collective-permute-start | bytes 786440 | tf_op jit(solution)/shard_map/ppermute | solution.py:28
  63.0 2.8 %copy-start.1 = (bf16[1024,1536]{1,0:T(8,128)(2,1)S(1)}, bf16[1024,1536]{1,0:T(8,128)(2,1)}, u32[]{:S(2)}) copy-start(bf16[1024,1536]{1,0:T(8,128)(2,1)} %refs_3_.1) | copy-start | bytes 9437188
